TPU v7x, 32 devices: a whole 2x2x4 slice. The times are simulated.
32 devices in a mesh: freq: 2 (over y), tm: 16 (over z, x, core).
Axes of the slice: x: 2, y: 2, z: 4, core: 2. Of those that a mesh axis runs over, the one named last changes fastest.
Arguments:
- tokens: bfloat16 [2, 8, 1024, 768], P(None, 'freq', 'tm'), may hold values from -6 to 6
- out_grad: bfloat16 [2, 8, 1024, 768], P(None, 'freq', 'tm'), may hold values from -6 to 6
- lengths: int32 [2], replicated, may hold values from 128 to 1024, as said below
- norm1_gain: float32 [768], replicated, may hold values from 0.1 to 1.9
- norm1_shift: float32 [768], replicated, may hold values from -1.75 to 1.75
- w_qkv: bfloat16 [768, 2304], replicated, may hold values from -0.21875 to 0.21875
- query_bias: float32 [768], replicated, may hold values from -3 to 3
- value_bias: float32 [768], replicated, may hold values from -0.125 to 0.125
- w_proj: bfloat16 [768, 768], replicated, may hold values from -6 to 6
- proj_bias: float32 [768], replicated, may hold values from -1.75 to 1.75
- norm2_gain: float32 [768], replicated, may hold values from 0.1 to 1.9
- norm2_shift: float32 [768], replicated, may hold values from -1.75 to 1.75
- w_fc1: bfloat16 [768, 3072], replicated, may hold values from -0.21875 to 0.21875
- fc1_bias: float32 [3072], replicated, may hold values from -3 to 3
- w_fc2: bfloat16 [3072, 768], replicated, may hold values from -0.109375 to 0.109375
- fc2_bias: float32 [768], replicated, may hold values from -1.75 to 1.75
- moment: float32 [7090176], P(('freq', 'tm'))
- ema_decay: float32 [1], replicated, may hold values from 0.5 to 0.95
Outputs:
- mixed: bfloat16 [2, 8, 1024, 768], P(None, 'freq', 'tm')
- input_grad: bfloat16 [2, 8, 1024, 768], P(None, 'freq', 'tm')
- weight_grad: float32 [7090176], P(('freq', 'tm'))
- new_moment: float32 [7090176], P(('freq', 'tm'))
Inputs may be any that keep to these rules, and one draw needn't show every extreme that they name: `lengths`: at least one clip slot, drawn from the seed, is 1024 frames long.
All inputs are finite; a program needn't handle non-finite values.
Results may differ from a plain program's by a relative error of at most 0.013.
Values may be sent and summed in bfloat16 or wider, within the bound.
No kernel may reach another device: no remote copies, remote signals or barrier semaphores. Data moves between devices by JAX's collectives and lax.ppermute only.
A program may use at most 512 MiB of HBM per device.

v0:
```python
import functools
import math

import jax
import jax.numpy as jnp
from jax import lax
from jax.experimental import pallas as pl
from jax.experimental.pallas import tpu as pltpu
from jax.sharding import Mesh
from jax.sharding import PartitionSpec as P

HEADS = 12
HEAD_DIM = 64
GROUPS = 4
GROUP_HEADS = HEADS // GROUPS
PAIR = 2 * HEAD_DIM
LANES = 128
OUT_ROWS = HEAD_DIM + 8
GRAD_ROWS = HEAD_DIM + 16
EPSILON = 1e-06
NEGATIVE = -1e30
LOG2E = math.log2(math.e)
LN2 = math.log(2.0)
SCALE = HEAD_DIM**-0.5
VMEM_LIMIT = 60 * 2**20
BF16 = jnp.bfloat16
F32 = jnp.float32


def dot32(left, right, contract):
    return lax.dot_general(left, right, ((contract[:1], contract[1:]), ((), ())), preferred_element_type=F32)


def work(info_ref, clip, times):
    t, full, rest = info_ref[1], info_ref[2 + 2 * clip], info_ref[3 + 2 * clip]
    live = full + (rest > 0).astype(jnp.int32)
    query_blocks = (live + times - 1) // times
    key_blocks = jnp.maximum(full - t + times - 1, 0) // times
    partial = (rest > 0) & (full % times == t)
    return query_blocks, key_blocks, partial, rest


def joined(ref, late):
    tiles = [ref[late, j] for j in range(ref.shape[1])]
    return tiles[0] if len(tiles) == 1 else jnp.concatenate(tiles, axis=1)


def load_pairs(kv_refs, slot):
    return [ref[f, slot, 0] for ref in kv_refs for f in range(ref.shape[0])]


def attend_kernel(clip, times, frames, n_kv, n_q, n_out, info_ref, *refs):
    kv_refs, q_refs, refs = refs[:n_kv], refs[n_kv : n_kv + n_q], refs[n_kv + n_q :]
    refs = refs[-n_out - 5 :]
    out_refs, (acc, top, q_pad, scores, tops) = refs[:n_out], refs[n_out:]
    query_blocks, key_blocks, partial, rest = work(info_ref, clip, times)
    width = q_refs[0].shape[1] * q_refs[0].shape[3]
    rows = scores.shape[1]
    for late in range(GROUPS):
        for p, ref in enumerate(q_refs):
            q_pad[late, :HEAD_DIM, p * width : (p + 1) * width] = joined(ref, late)
        q_pad[late, HEAD_DIM:, :] = jnp.zeros((HEAD_DIM, q_pad.shape[2]), BF16)
    acc[...] = jnp.zeros_like(acc)
    top[...] = jnp.full_like(top, NEGATIVE)
    ones = jnp.ones((16, rows), BF16)

    def load(block):
        return jnp.concatenate(load_pairs(kv_refs, block), axis=0)

    def consume(u, pair, block_scores, block_top):
        old = top[u]
        new = jnp.maximum(old, block_top)
        probs = jnp.exp2(block_scores - new).astype(BF16)
        top[u] = new
        values = jnp.concatenate([pair.T[HEAD_DIM:], ones], axis=0)
        acc[u] = acc[u] * jnp.exp2(old - new) + dot32(values, probs, (1, 0))

    def masked(u, _):
        pair = load(key_blocks)
        alive = lax.broadcasted_iota(jnp.int32, (rows, 1), 0) % frames < rest
        block_scores = jnp.where(alive, dot32(pair, q_pad[u], (1, 0)), NEGATIVE)
        consume(u, pair, block_scores, jnp.max(block_scores, axis=0, keepdims=True))
        return 0

    lax.fori_loop(0, jnp.where(partial, query_blocks, 0), masked, 0)
    total = query_blocks * key_blocks
    per = jnp.maximum(key_blocks, 1)

    def score(step, slot):
        block_scores = dot32(load(step % per), q_pad[step // per], (1, 0))
        scores[slot] = block_scores
        tops[slot] = jnp.max(block_scores, axis=0, keepdims=True)

    @pl.when(total > 0)
    def _():
        score(0, 0)

    def two_steps(double, _):
        for slot in range(2):
            step = 2 * double + slot
            score(jnp.minimum(step + 1, total - 1), 1 - slot)
            consume(step // per, load(step % per), scores[slot], tops[slot])
        return 0

    lax.fori_loop(0, total // 2, two_steps, 0)

    @pl.when(total % 2 == 1)
    def _():
        consume((total - 1) // per, load((total - 1) % per), scores[0], tops[0])

    for late in range(GROUPS):
        norm = acc[late, HEAD_DIM : HEAD_DIM + 1, :]
        some = norm > 0.0
        safe = jnp.where(some, norm, 1.0)
        out = acc[late, :HEAD_DIM, :] / safe
        lse = jnp.where(some, top[late] + jnp.log2(safe), NEGATIVE)
        p = 0
        for ref in out_refs:
            for part in range(ref.shape[0]):
                cols = slice(p * width, (p + 1) * width)
                ref[part, late, :HEAD_DIM, :] = out[:, cols]
                ref[part, late, HEAD_DIM:, :] = jnp.broadcast_to(lse[:, cols], (OUT_ROWS - HEAD_DIM, width))
                p += 1


def specs_of(kv, q, clip, clips):
    kv_specs = [pl.BlockSpec((a.shape[0], GROUPS, 1, *a.shape[3:]), lambda i, *_: (0, 0, clip, 0, 0)) for a in kv]
    _, tiles, _, lanes = q[0].shape
    q_specs = [pl.BlockSpec((GROUPS, tiles // clips, HEAD_DIM, lanes), lambda i, *_: (0, clip, 0, 0)) for a in q]
    return kv_specs, q_specs, tiles * lanes // clips


def attend(info, kv, q, clip, clips, times, frames, parts, before, after):
    kv_specs, q_specs, width = specs_of(kv, q, clip, clips)
    queries = len(q) * width
    rows = sum(a.shape[0] for a in kv) * kv[0].shape[3]
    pairs = GROUPS * rows * GROUPS * queries
    out_specs = [pl.BlockSpec((n, GROUPS, OUT_ROWS, width), lambda i, *_: (0, 0, 0, clip)) for n in parts]
    n_in = 1 + len(kv) + len(q)
    return pl.pallas_call(
        functools.partial(attend_kernel, clip, times, frames, len(kv), len(q), len(parts)),
        grid_spec=pltpu.PrefetchScalarGridSpec(
            num_scalar_prefetch=1,
            grid=(1,),
            in_specs=kv_specs + q_specs + [pl.BlockSpec(memory_space=pl.ANY)] * (len(before) + len(after)),
            out_specs=out_specs,
            scratch_shapes=[
                pltpu.VMEM((GROUPS, GRAD_ROWS, queries), F32),
                pltpu.VMEM((GROUPS, 1, queries), F32),
                pltpu.VMEM((GROUPS, PAIR, queries), BF16),
                pltpu.VMEM((2, rows, queries), F32),
                pltpu.VMEM((2, 1, queries), F32),
            ],
        ),
        out_shape=[jax.ShapeDtypeStruct((n, GROUPS, OUT_ROWS, clips * width), F32) for n in parts],
        input_output_aliases={n_in + i: i for i in range(len(before))},
        compiler_params=pltpu.CompilerParams(vmem_limit_bytes=VMEM_LIMIT),
        cost_estimate=pl.CostEstimate(flops=256 * pairs, bytes_accessed=pairs // 16, transcendentals=pairs),
    )(info, *kv, *q, *before, *after)


def attend_back_kernel(clip, times, frames, cuts, n_kv, n_q, n_out, info_ref, *refs):
    kv_refs, q_refs, grad_refs = refs[:n_kv], refs[n_kv : n_kv + n_q], refs[n_kv + n_q : n_kv + 2 * n_q]
    refs = refs[-n_out - n_kv - 8 :]
    back_q_refs, back_kv_refs, refs = refs[:n_out], refs[n_out : n_out + n_kv], refs[n_out + n_kv :]
    back_q, back_kv, q_cols, grad_cols, q_rows, grad_rows, lse, delta = refs
    query_blocks, key_blocks, partial, rest = work(info_ref, clip, times)
    width = grad_refs[0].shape[-1]
    part_rows = kv_refs[0].shape[3]
    rows = back_kv.shape[1]
    cut = rows // cuts
    zero = jnp.zeros((HEAD_DIM, width), BF16)

    def prepare(late, _):
        for p, (q_ref, grad_ref) in enumerate(zip(q_refs, grad_refs)):
            cols = slice(p * width, (p + 1) * width)
            query = jnp.concatenate([joined(q_ref, late), zero], axis=0)
            grad = jnp.concatenate([zero, grad_ref[late, :HEAD_DIM]], axis=0)
            q_cols[late, :, cols] = query
            grad_cols[late, :, cols] = grad
            q_rows[late, cols, :] = query.T
            grad_rows[late, cols, :] = grad.T
            extra = grad_ref[late, HEAD_DIM:].astype(F32)
            lse[late, :, cols] = extra[0:1] + extra[1:2] + extra[2:3]
            delta[late, :, cols] = extra[3:4] + extra[4:5] + extra[5:6]
        return 0

    lax.fori_loop(0, query_blocks, prepare, 0)
    back_q[...] = jnp.zeros_like(back_q)
    back_kv[...] = jnp.zeros_like(back_kv)

    def step(u, block, masked):
        pairs = load_pairs(kv_refs, block)
        for k in range(cuts):
            part = pairs[k * len(pairs) // cuts : (k + 1) * len(pairs) // cuts]
            pair = part[0] if len(part) == 1 else jnp.concatenate(part, axis=0)
            probs = jnp.exp2(dot32(pair, q_cols[u], (1, 0)) - lse[u])
            if masked:
                row = lax.broadcasted_iota(jnp.int32, (cut, 1), 0)
                probs = jnp.where(row % frames < rest, probs, 0.0)
            back_probs = dot32(pair, grad_cols[u], (1, 0))
            back_scores = (probs * (back_probs - delta[u])).astype(BF16)
            back_pair = dot32(probs.astype(BF16), grad_rows[u], (1, 0)) + dot32(back_scores, q_rows[u], (1, 0))
            back_q[u] += dot32(pair, back_scores, (0, 0))
            back_kv[block, k * cut : (k + 1) * cut, :] += back_pair
        return 0

    lax.fori_loop(0, jnp.where(partial, query_blocks, 0), lambda u, _: step(u, key_blocks, True), 0)
    per = jnp.maximum(key_blocks, 1)
    lax.fori_loop(0, query_blocks * key_blocks, lambda i, _: step(i // per, i % per, False), 0)
    is_key = lax.broadcasted_iota(jnp.int32, (1, PAIR), 1) < HEAD_DIM
    factor = jnp.where(is_key, jnp.float32(LN2), jnp.float32(1.0))
    for late in range(GROUPS):
        p = 0
        for ref in back_q_refs:
            for part in range(ref.shape[0]):
                cols = slice(p * width, (p + 1) * width)
                ref[part, late] = (back_q[late, :HEAD_DIM, cols] * SCALE).astype(BF16)
                p += 1
        p = 0
        for ref in back_kv_refs:
            for f in range(ref.shape[0]):
                ref[f, late, 0] = (back_kv[late, p * part_rows : (p + 1) * part_rows, :] * factor).astype(BF16)
                p += 1


def attend_back(info, kv, q, grad, clip, clips, times, frames, parts, before, after):
    kv_specs, q_specs, width = specs_of(kv, q, clip, clips)
    queries = len(q) * width
    rows = sum(a.shape[0] for a in kv) * kv[0].shape[3]
    pairs = GROUPS * rows * GROUPS * queries
    grad_specs = [pl.BlockSpec((GROUPS, GRAD_ROWS, width), lambda i, *_: (0, 0, clip)) for a in grad]
    q_out = [pl.BlockSpec((n, GROUPS, HEAD_DIM, width), lambda i, *_: (0, 0, 0, clip)) for n in parts]
    n_in = 1 + len(kv) + len(q) + len(grad)
    return pl.pallas_call(
        functools.partial(attend_back_kernel, clip, times, frames, 2, len(kv), len(q), len(parts)),
        grid_spec=pltpu.PrefetchScalarGridSpec(
            num_scalar_prefetch=1,
            grid=(1,),
            in_specs=kv_specs + q_specs + grad_specs + [pl.BlockSpec(memory_space=pl.ANY)] * (len(before) + len(after)),
            out_specs=q_out + kv_specs,
            scratch_shapes=[
                pltpu.VMEM((GROUPS, PAIR, queries), F32),
                pltpu.VMEM((GROUPS, rows, PAIR), F32),
                pltpu.VMEM((GROUPS, PAIR, queries), BF16),
                pltpu.VMEM((GROUPS, PAIR, queries), BF16),
                pltpu.VMEM((GROUPS, queries, PAIR), BF16),
                pltpu.VMEM((GROUPS, queries, PAIR), BF16),
                pltpu.VMEM((GROUPS, 1, queries), F32),
                pltpu.VMEM((GROUPS, 1, queries), F32),
            ],
        ),
        out_shape=[jax.ShapeDtypeStruct((n, GROUPS, HEAD_DIM, clips * width), BF16) for n in parts]
        + [jax.ShapeDtypeStruct(a.shape, BF16) for a in kv],
        input_output_aliases={n_in + i: i for i in range(len(before))},
        compiler_params=pltpu.CompilerParams(vmem_limit_bytes=VMEM_LIMIT),
        cost_estimate=pl.CostEstimate(flops=640 * pairs, bytes_accessed=pairs // 8, transcendentals=pairs),
    )(info, *kv, *q, *grad, *before, *after)


def thirds(values):
    high = values.astype(BF16).astype(F32)
    middle = (values - high).astype(BF16).astype(F32)
    return jnp.concatenate([high, middle, values - high - middle], axis=0)


def blend(left, left_lse, right, right_lse):
    most = jnp.maximum(left_lse, right_lse)
    left_part, right_part = jnp.exp2(left_lse - most), jnp.exp2(right_lse - most)
    total = left_part + right_part
    return (left * left_part + right * right_part) / total, most + jnp.log2(total)


def merge_cores_kernel(kept_ref, came_ref, mine_ref, sent_ref):
    for n in range(GROUPS):
        for part in range(2):
            left, right = kept_ref[part, n], came_ref[part, n]
            out, lse = blend(left[:HEAD_DIM], left[HEAD_DIM : HEAD_DIM + 1], right[:HEAD_DIM], right[HEAD_DIM : HEAD_DIM + 1])
            if part == 0:
                mine_ref[n, :HEAD_DIM] = out
                mine_ref[n, HEAD_DIM:] = jnp.broadcast_to(lse, (OUT_ROWS - HEAD_DIM, out.shape[1]))
            else:
                fill = jnp.zeros((GRAD_ROWS - HEAD_DIM - 3, out.shape[1]), F32)
                sent_ref[n] = jnp.concatenate([out, thirds(lse), fill], axis=0).astype(BF16)


def merge_cores(kept, came):
    _, _, _, width = kept.shape
    return pl.pallas_call(
        merge_cores_kernel,
        out_shape=[jax.ShapeDtypeStruct((GROUPS, OUT_ROWS, width), F32), jax.ShapeDtypeStruct((GROUPS, GRAD_ROWS, width), BF16)],
        compiler_params=pltpu.CompilerParams(vmem_limit_bytes=VMEM_LIMIT),
    )(kept, came)


def merge_chips_kernel(mine_ref, came_ref, out_ref, low_ref):
    for n in range(GROUPS):
        left, right = mine_ref[n], came_ref[n].astype(F32)
        right_lse = right[HEAD_DIM : HEAD_DIM + 1] + right[HEAD_DIM + 1 : HEAD_DIM + 2] + right[HEAD_DIM + 2 : HEAD_DIM + 3]
        out, lse = blend(left[:HEAD_DIM], left[HEAD_DIM : HEAD_DIM + 1], right[:HEAD_DIM], right_lse)
        low_ref[n] = out.astype(BF16)
        out_ref[n, :HEAD_DIM] = out
        out_ref[n, HEAD_DIM:] = jnp.broadcast_to(lse, (OUT_ROWS - HEAD_DIM, out.shape[1]))


def merge_chips(mine, came):
    _, _, width = mine.shape
    return pl.pallas_call(
        merge_chips_kernel,
        out_shape=[jax.ShapeDtypeStruct((GROUPS, OUT_ROWS, width), F32)] + [jax.ShapeDtypeStruct((GROUPS, HEAD_DIM, width), BF16)],
        compiler_params=pltpu.CompilerParams(vmem_limit_bytes=VMEM_LIMIT),
    )(mine, came)


def grad_rows_kernel(grad_ref, *refs):
    out_refs, ready_refs = refs[:GROUP_HEADS], refs[-GROUP_HEADS:]
    for head in range(GROUP_HEADS):
        for n in range(GROUPS):
            grad = grad_ref[n, head * HEAD_DIM : (head + 1) * HEAD_DIM].astype(F32)
            out = out_refs[head][n]
            delta = jnp.sum(grad * out[:HEAD_DIM], axis=0, keepdims=True)
            fill = jnp.zeros((GRAD_ROWS - HEAD_DIM - 6, grad.shape[1]), F32)
            rows = jnp.concatenate([grad, thirds(out[HEAD_DIM : HEAD_DIM + 1]), thirds(delta), fill], axis=0)
            ready_refs[head][n] = rows.astype(BF16)


def grad_rows_of(grad, outs, after):
    width = grad.shape[-1]
    whole = pl.BlockSpec(memory_space=pltpu.VMEM)
    return pl.pallas_call(
        grad_rows_kernel,
        in_specs=[whole] * (1 + len(outs)) + [pl.BlockSpec(memory_space=pl.ANY)],
        out_shape=[jax.ShapeDtypeStruct((GROUPS, GRAD_ROWS, width), BF16)] * GROUP_HEADS,
        compiler_params=pltpu.CompilerParams(vmem_limit_bytes=VMEM_LIMIT),
    )(grad, *outs, after)


def sum_back_kernel(kept_ref, came_ref, q_kept_ref, q_came_ref, ready_ref):
    rows = kept_ref.shape[1]
    for n in range(GROUPS):
        ready_ref[n, :rows] = (kept_ref[n].astype(F32) + came_ref[n].astype(F32)).astype(BF16)
        query = (q_kept_ref[n].astype(F32) + q_came_ref[n].astype(F32)).astype(BF16)
        for j in range(rows // LANES):
            at = rows + j * HEAD_DIM
            ready_ref[n, at : at + HEAD_DIM] = query[:, j * LANES : (j + 1) * LANES]


def sum_back(kept, came, q_kept, q_came):
    groups, rows, _ = kept.shape
    return pl.pallas_call(
        sum_back_kernel,
        out_shape=jax.ShapeDtypeStruct((groups, rows + rows // LANES * HEAD_DIM, LANES), BF16),
        compiler_params=pltpu.CompilerParams(vmem_limit_bytes=VMEM_LIMIT),
    )(kept, came, q_kept, q_came)


def spread(lines, at, stride, values):
    rows, width = values.shape
    for piece in range(width // LANES):
        lines[pl.ds(at + piece, rows, stride=stride), :] = values[:, piece * LANES : (piece + 1) * LANES]


def write_window(start, lines, ref, at=0):
    skip = start % 8
    rows = ref.shape[1]
    base = pl.multiple_of(start - skip, 8)
    for s in range(8):

        @pl.when(skip == s)
        def _():
            ref[at] = lines[pl.ds(base, rows + 8), :][s : s + rows].astype(BF16)


def pack_early_kernel(size, first, att_ref, branch_ref, normed_ref, pre_ref, act_ref, out_ref, vec_ref, window_ref, lines):
    step = pl.program_id(0)

    @pl.when(step == 0)
    def _():
        width = branch_ref.shape[1]
        blocks = pre_ref.shape[1] // width
        per = width // LANES
        spread(lines, 0, per, dot32(att_ref[...], branch_ref[...], (1, 0)))
        at = width * per
        lines[at : at + 3 * per, :] = vec_ref[0 : 3 * per]
        at += 3 * per
        for b in range(blocks):
            cols = slice(b * width, (b + 1) * width)
            spread(lines, at + b * per, blocks * per, dot32(normed_ref[...], pre_ref[:, cols], (0, 0)))
        at += blocks * width * per
        lines[at : at + blocks * per, :] = vec_ref[3 * per : (3 + blocks) * per]
        at += blocks * per
        for b in range(blocks):
            cols = slice(b * width, (b + 1) * width)
            spread(lines, at + b * width * per, per, dot32(act_ref[:, cols], out_ref[...], (0, 0)))
        at += blocks * width * per
        lines[at : at + per, :] = vec_ref[(3 + blocks) * per :]
        lines[at + per :, :] = jnp.zeros((lines.shape[0] - at - per, LANES), F32)

    @pl.when(step < first)
    def _():
        window_ref[...] = jnp.zeros_like(window_ref)

    @pl.when(step >= first)
    def _():
        write_window((step - first) * size, lines, window_ref)


def pack_early(devices, size, *operands):
    chunks = devices - LATE_CHUNKS
    whole = [pl.BlockSpec(a.shape, lambda j: (0, 0)) for a in operands]
    entries = chunks * size * LANES
    return pl.pallas_call(
        functools.partial(pack_early_kernel, size, LATE_CHUNKS),
        grid=(devices,),
        in_specs=whole,
        out_specs=pl.BlockSpec((1, EARLY_WINDOW, LANES), lambda j: (j, 0, 0)),
        scratch_shapes=[pltpu.VMEM((-(-(chunks - 1) * size // 8) * 8 + EARLY_WINDOW + 8, LANES), F32)],
        out_shape=jax.ShapeDtypeStruct((devices, EARLY_WINDOW, LANES), BF16),
        compiler_params=pltpu.CompilerParams(vmem_limit_bytes=VMEM_LIMIT),
        cost_estimate=pl.CostEstimate(flops=1024 * entries, bytes_accessed=4 * entries, transcendentals=0),
    )(*operands)


SWAP = [(0, 1), (1, 0)]


def swap(values, axis):
    return lax.ppermute(values, axis, SWAP)


def add(left, right):
    return (left.astype(F32) + right.astype(F32)).astype(BF16)


def trade(values, dim, keep, axis):
    sent = lax.dynamic_index_in_dim(values, 1 - keep, dim, keepdims=False)
    kept = lax.dynamic_index_in_dim(values, keep, dim, keepdims=False)
    return add(kept, swap(sent, axis))


EARLY_WINDOW = 1744
LATE_CHUNKS = 8
LATE_WINDOW = 1792


def reduce_late(send, keep):
    f, g, x = lax.axis_index("f"), lax.axis_index("g"), lax.axis_index("x")
    pairs = add(keep, swap(send, "c")).reshape(2, 2, 4, -1, LANES)
    first = trade(trade(pairs[:, :, :2], 1, x, "x"), 1, f, "f")
    second = trade(trade(pairs[:, :, 2:], 2, f, "f"), 1, x, "x")
    mine = jnp.concatenate([first, second], axis=1)
    low = jnp.minimum(g, 1)
    near = add(mine, lax.ppermute(mine, "g", [(3, 2)]))
    far = lax.ppermute(near, "g", [(2, 1)])
    mine = jnp.where(g == 1, add(mine, far), mine)
    sent = lax.dynamic_index_in_dim(mine, 1 - low, 0, keepdims=False)
    mine = lax.dynamic_index_in_dim(mine, low, 0, keepdims=False)
    mine = add(mine, lax.ppermute(sent, "g", SWAP))
    far = swap(mine, "f")
    part = LATE_WINDOW // 4
    return jnp.concatenate([mine[:part], far[:part], mine[part:], far[part:]], axis=0).astype(F32)


def own_chunk(early, late, size):
    is_late = (lax.axis_index("f") == 0) & (lax.axis_index("g") < 2)
    return jnp.where(is_late, late[: size // LANES], early[: size // LANES]).reshape(size)


def centre(values):
    centred = values - jnp.mean(values, axis=-1, keepdims=True)
    scale = lax.rsqrt(jnp.mean(centred * centred, axis=-1, keepdims=True) + EPSILON)
    return centred * scale, scale


def centre_back(grad, unit, scale):
    mean = jnp.mean(grad, axis=-1, keepdims=True)
    along = jnp.mean(grad * unit, axis=-1, keepdims=True)
    return scale * (grad - mean - unit * along)


def row(ref):
    return ref[...].reshape(1, -1)


def swap_halves(values):
    return pltpu.roll(values, HEAD_DIM, axis=1)


def start_kernel(info_ref, x_ref, gain_ref, shift_ref, w_ref, query_bias_ref, value_bias_ref, *refs):
    rows, width = x_ref.shape

    def put(head, values):
        refs[head % GROUP_HEADS][head // GROUP_HEADS, :rows] = values.astype(BF16)

    unit, _ = centre(x_ref[...].astype(F32))
    normed = (unit * row(gain_ref) + row(shift_ref)).astype(BF16)
    keys = dot32(normed, w_ref[:, width : 2 * width], (1, 0))
    values = dot32(normed, w_ref[:, 2 * width :], (1, 0)) + row(value_bias_ref)
    is_key = lax.broadcasted_iota(jnp.int32, (1, PAIR), 1) < HEAD_DIM
    for j in range(HEADS // 2):
        key, value = keys[:, j * PAIR : (j + 1) * PAIR], values[:, j * PAIR : (j + 1) * PAIR]
        put(2 * j, jnp.where(is_key, key, swap_halves(value)))
        put(2 * j + 1, jnp.where(is_key, swap_halves(key), value))
    query = (dot32(normed, w_ref[:, :width], (1, 0)) + row(query_bias_ref)) * (SCALE * LOG2E)
    query = query.astype(BF16).T
    for head in range(HEADS):
        part = query[head * HEAD_DIM : (head + 1) * HEAD_DIM]
        for tile in range(rows // LANES):
            at = rows + tile * HEAD_DIM
            refs[head % GROUP_HEADS][head // GROUP_HEADS, at : at + HEAD_DIM] = part[:, tile * LANES : (tile + 1) * LANES]


def one_step(kernel, info, operands, shapes, scratch, flops):
    return pl.pallas_call(
        kernel,
        grid_spec=pltpu.PrefetchScalarGridSpec(
            num_scalar_prefetch=1,
            grid=(1,),
            in_specs=[pl.BlockSpec(a.shape, lambda i, *_, n=a.ndim: (0,) * n) for a in operands],
            out_specs=[pl.BlockSpec(a.shape, lambda i, *_, n=len(a.shape): (0,) * n) for a in shapes],
            scratch_shapes=scratch,
        ),
        out_shape=shapes,
        compiler_params=pltpu.CompilerParams(vmem_limit_bytes=VMEM_LIMIT),
        cost_estimate=pl.CostEstimate(flops=flops, bytes_accessed=flops // 500, transcendentals=0),
    )(info, *operands)


def start(info, x, gain, shift, w_qkv, query_bias, value_bias):
    rows, width = x.shape
    shapes = [jax.ShapeDtypeStruct((GROUPS, rows + rows // LANES * HEAD_DIM, LANES), BF16)] * GROUP_HEADS
    operands = (x, gain, shift, w_qkv, query_bias, value_bias)
    return one_step(start_kernel, info, operands, shapes, [], 2 * rows * width * 3 * width)


def middle_kernel(
    info_ref, x_ref, out_grad_ref, keep_ref, w_proj_ref, proj_bias_ref, gain_ref, shift_ref, w_fc1_ref, fc1_bias_ref, w_fc2_ref,
    fc2_bias_ref, *refs,
):
    attended_refs, refs = refs[:GROUP_HEADS], refs[GROUP_HEADS:]
    mixed_ref, back_hidden_ref, att_ref, branch_ref, normed_ref, pre_ref, act_ref, out_ref, vec_ref = refs[:9]
    grad_ref, heads = refs[9:]
    width = x_ref.shape[1]
    rows = x_ref.shape[0]
    per = width // LANES
    for head in range(HEADS):
        heads[head] = attended_refs[head % GROUP_HEADS][head // GROUP_HEADS]
    attended = heads[...].reshape(width, rows)
    att_ref[...] = attended
    keep = keep_ref[...]
    hidden = x_ref[...].astype(F32) + (dot32(attended, w_proj_ref[...], (0, 0)) + row(proj_bias_ref))
    unit, scale = centre(hidden)
    normed = (unit * row(gain_ref) + row(shift_ref)).astype(BF16)
    normed_ref[...] = normed
    grad_out = out_grad_ref[...].astype(F32) * keep
    low_out = grad_out.astype(BF16)
    out_ref[...] = low_out
    branch2 = jnp.zeros((rows, width), F32)
    back_normed = jnp.zeros((rows, width), F32)

    def put(at, line):
        for piece in range(line.shape[1] // LANES):
            vec_ref[at + piece : at + piece + 1, :] = line[:, piece * LANES : (piece + 1) * LANES]

    blocks = pre_ref.shape[1] // width
    for b in range(blocks):
        cols = slice(b * width, (b + 1) * width)
        pre = dot32(normed, w_fc1_ref[:, cols], (1, 0)) + row(fc1_bias_ref)[:, cols]
        share = 0.5 * (1.0 + lax.erf(pre * (0.5**0.5)))
        low_act = (pre * share).astype(BF16)
        act_ref[:, cols] = low_act
        branch2 += dot32(low_act, w_fc2_ref[cols, :], (1, 0))
        slope = share + pre * jnp.exp(-0.5 * pre * pre) * ((2.0 * math.pi) ** -0.5)
        back_pre = (dot32(low_out, w_fc2_ref[cols, :], (1, 1)) * slope).astype(BF16)
        pre_ref[:, cols] = back_pre
        put((3 + b) * per, jnp.sum(back_pre.astype(F32), axis=0, keepdims=True))
        back_normed += dot32(back_pre, w_fc1_ref[:, cols], (1, 1))
    mixed_ref[...] = ((hidden + (branch2 + row(fc2_bias_ref))) * keep).astype(BF16)
    put((3 + blocks) * per, jnp.sum(low_out.astype(F32), axis=0, keepdims=True))
    put(per, jnp.sum(back_normed * unit, axis=0, keepdims=True))
    put(2 * per, jnp.sum(back_normed, axis=0, keepdims=True))
    back_hidden = grad_out + centre_back(back_normed * row(gain_ref), unit, scale)
    back_hidden_ref[...] = back_hidden
    branch = back_hidden.astype(BF16)
    branch_ref[...] = branch
    put(0, jnp.sum(branch.astype(F32), axis=0, keepdims=True))
    back_attended = dot32(w_proj_ref[...], branch, (1, 1)).astype(BF16)
    grad_ref[...] = back_attended.reshape(grad_ref.shape)


def middle(info, x, out_grad, keep, w_proj, proj_bias, gain, shift, w_fc1, fc1_bias, w_fc2, fc2_bias, attended):
    rows, width = x.shape
    ff = w_fc1.shape[1]
    low = lambda *shape: jax.ShapeDtypeStruct(shape, BF16)
    shapes = [
        low(rows, width), jax.ShapeDtypeStruct((rows, width), F32), low(width, rows), low(rows, width), low(rows, width),
        low(rows, ff), low(rows, ff), low(rows, width), jax.ShapeDtypeStruct(((4 * width + ff) // LANES, LANES), F32),
        low(GROUPS, width // GROUPS, rows),
    ]
    operands = [x, out_grad, keep, w_proj, proj_bias, gain, shift, w_fc1, fc1_bias, w_fc2, fc2_bias]
    operands += attended
    scratch = [pltpu.VMEM((HEADS, HEAD_DIM, rows), BF16)]
    outs = one_step(middle_kernel, info, operands, shapes, scratch, 2 * rows * width * (2 * width + 4 * ff))
    return outs[0], outs[1], outs[2:9], outs[9]


def finish_kernel(size, info_ref, x_ref, gain_ref, shift_ref, w_ref, back_hidden_ref, *refs):
    back_refs, (input_ref, send_ref, keep_ref, queries, flat, lines) = refs[:GROUP_HEADS], refs[GROUP_HEADS:]
    rows, width = x_ref.shape
    per = width // LANES

    def pair(head):
        return back_refs[head % GROUP_HEADS][head // GROUP_HEADS, :rows].astype(F32)

    for head in range(HEADS):
        ref = back_refs[head % GROUP_HEADS]
        for tile in range(rows // LANES):
            at = rows + tile * HEAD_DIM
            queries[head, :, tile * LANES : (tile + 1) * LANES] = ref[head // GROUP_HEADS, at : at + HEAD_DIM]
    is_key = lax.broadcasted_iota(jnp.int32, (1, PAIR), 1) < HEAD_DIM
    for j in range(HEADS // 2):
        first, second = pair(2 * j), pair(2 * j + 1)
        flat[:, j * PAIR : (j + 1) * PAIR] = jnp.where(is_key, first, swap_halves(second)).astype(BF16)
        flat[:, width + j * PAIR : width + (j + 1) * PAIR] = jnp.where(is_key, swap_halves(first), second).astype(BF16)
    query = queries[...].reshape(width, rows)
    unit, scale = centre(x_ref[...].astype(F32))
    normed = (unit * row(gain_ref) + row(shift_ref)).astype(BF16)
    spread(lines, 2 * per, 3 * per, dot32(normed, query, (0, 1)))
    for b in range(2):
        spread(lines, (3 + b) * per, 3 * per, dot32(normed, flat[:, b * width : (b + 1) * width], (0, 0)))
    back_normed = dot32(query, w_ref[:, :width], (0, 1)) + dot32(flat[...], w_ref[:, width:], (1, 1))
    input_ref[...] = (back_hidden_ref[...] + centre_back(back_normed * row(gain_ref), unit, scale)).astype(BF16)

    def put(at, line):
        for piece in range(per):
            lines[at + piece : at + piece + 1, :] = line[:, piece * LANES : (piece + 1) * LANES]

    put(0, jnp.sum(back_normed * unit, axis=0, keepdims=True))
    put(per, jnp.sum(back_normed, axis=0, keepdims=True))
    at = (2 + 3 * width) * per
    put(at, dot32(jnp.ones((8, rows), BF16), query, (1, 1))[0:1])
    put(at + per, jnp.sum(flat[:, width:].astype(F32), axis=0, keepdims=True))
    lines[at + 2 * per :, :] = jnp.zeros((lines.shape[0] - at - 2 * per, LANES), F32)
    core = info_ref[1] % 2

    def window(step, _):
        for ref, which in ((send_ref, 1 - core), (keep_ref, core)):
            write_window((2 * step + which) * size, lines, ref, step)
        return 0

    lax.fori_loop(0, LATE_CHUNKS // 2, window, 0)


def finish(size, info, x, gain, shift, w_qkv, back_hidden, back):
    rows, width = x.shape
    window = jax.ShapeDtypeStruct((LATE_CHUNKS // 2, LATE_WINDOW, LANES), BF16)
    shapes = [jax.ShapeDtypeStruct((rows, width), BF16), window, window]
    operands = [x, gain, shift, w_qkv, back_hidden, *back]
    scratch = [
        pltpu.VMEM((HEADS, HEAD_DIM, rows), BF16),
        pltpu.VMEM((rows, 2 * width), BF16),
        pltpu.VMEM((-(-(LATE_CHUNKS - 1) * size // 8) * 8 + LATE_WINDOW + 8, LANES), F32),
    ]
    kernel = functools.partial(finish_kernel, size)
    return one_step(kernel, info, operands, shapes, scratch, 4 * rows * width * 3 * width)


def along_g(values):
    return lax.all_to_all(values, "g", 0, 0, tiled=True)


def hold(values, after):
    return lax.optimization_barrier((values, list(after)))[0] if len(after) > 0 else values


class Plane:
    parts = (2, 2)

    def gather_keys(self, kv):
        return [kv[None], swap(kv, "f")[None]]

    def gather_queries(self, q):
        over = swap(q, "x")
        return [q, over, swap(q, "c"), swap(over, "c")]

    gather_grads = gather_queries

    def merge(self, outs):
        mine, sent = merge_cores(outs[0], swap(outs[1], "c"))
        yield [sent]
        yield merge_chips(mine, swap(sent, "x"))

    def sum_back(self, outs):
        q_sent, q_kept, sent, kept = outs[1], outs[0], outs[3][0], outs[2][0]
        both = add(q_kept, swap(q_sent, "c"))
        groups, clips, rows, _ = kept.shape
        came = swap(sent, "f").reshape(groups, clips * rows, PAIR)
        return sum_back(kept.reshape(groups, clips * rows, PAIR), came, both[0], swap(both[1], "x"))


class AnyPlane:
    parts = (1,)

    def __init__(self, clips, times):
        self.clips, self.times = clips, times

    def split(self, values):
        groups, rows, width = values.shape
        values = values.reshape(groups, rows, self.clips, self.times, -1).transpose(3, 0, 1, 2, 4)
        return values.reshape(self.times, groups, rows, width // self.times)

    def gather_keys(self, kv):
        return [lax.all_gather(kv, "f")]

    def gather_queries(self, q):
        groups, tiles, rows, lanes = q.shape
        q = lax.all_gather(q.transpose(0, 2, 1, 3).reshape(groups, rows, self.clips, -1), "t")
        return [q.transpose(1, 3, 2, 0, 4).reshape(groups, self.clips, rows, -1)]

    def gather_grads(self, values):
        groups, rows, _ = values.shape
        values = lax.all_gather(values.reshape(groups, rows, self.clips, -1), "t")
        return [values.transpose(1, 2, 3, 0, 4).reshape(groups, rows, -1)]

    def merge(self, outs):
        came = lax.all_to_all(self.split(outs[0][0]), "t", 0, 0, tiled=True)
        out, lse = came[:, :, :HEAD_DIM], came[:, :, HEAD_DIM : HEAD_DIM + 1]
        most = jnp.max(lse, axis=0)
        share = jnp.exp2(lse - most)
        total = jnp.sum(share, axis=0)
        out = jnp.sum(out * share, axis=0) / total
        lse = jnp.broadcast_to(most + jnp.log2(total), (GROUPS, OUT_ROWS - HEAD_DIM, out.shape[-1]))
        yield [out]
        yield jnp.concatenate([out, lse], axis=1), out.astype(BF16)

    def sum_back(self, outs):
        back_q = lax.psum_scatter(self.split(outs[0][0]), "t", scatter_dimension=0, tiled=False)
        back_kv = lax.psum_scatter(outs[1], "f", scatter_dimension=0, tiled=False).reshape(GROUPS, -1, PAIR)
        back_q = back_q.reshape(GROUPS, HEAD_DIM, -1, LANES).transpose(0, 2, 1, 3).reshape(GROUPS, -1, LANES)
        return jnp.concatenate([back_kv, back_q], axis=1)


def layer_norm(values, scaling, offset):
    row_mean = jnp.mean(values, axis=-1, keepdims=True)
    centred = values - row_mean
    spread = jnp.mean(centred * centred, axis=-1, keepdims=True)
    return centred * lax.rsqrt(spread + EPSILON) * scaling + offset


def gelu_exact(values):
    return jax.nn.gelu(values, approximate=False)


def per_device(
    time_axes,
    tokens,
    out_grad,
    lengths,
    norm1_gain,
    norm1_shift,
    w_qkv,
    query_bias,
    value_bias,
    w_proj,
    proj_bias,
    norm2_gain,
    norm2_shift,
    w_fc1,
    fc1_bias,
    w_fc2,
    fc2_bias,
    moment,
    ema_decay,
):
    clips, freq_rows, frames, width = tokens.shape
    part = freq_rows * frames
    rows = clips * part
    times = lax.axis_size(time_axes)
    devices = lax.axis_size("f") * GROUPS * times
    early_index = lax.axis_index(time_axes)
    fast = time_axes == ("x", "c")
    plane = Plane() if fast else AnyPlane(clips, times)
    core = lax.axis_index(time_axes[-1]).reshape(1)
    first_frame = (lax.axis_index("g") * times + early_index) * frames
    frame = first_frame + lax.broadcasted_iota(jnp.int32, (1, freq_rows, frames), 2)
    keep_rows = (frame < lengths[:, None, None]).astype(F32).reshape(rows, 1)
    info = [lax.axis_index("g"), early_index]
    for clip in range(clips):
        info += [lengths[clip] // frames, lengths[clip] % frames]
    info = jnp.stack(info).astype(jnp.int32)

    x = tokens.reshape(rows, width)
    packs = start(info, x, norm1_gain, norm1_shift, w_qkv, query_bias, value_bias)
    kv, q, attended, kept, merges, outs = [], [], [], [], [], ()

    def fetch(head, after):
        got = along_g(packs[head])
        pairs, queries = hold((got[:, :rows], got[:, rows:]), after)
        kv.append(plane.gather_keys(pairs.reshape(GROUPS, clips, part, PAIR)))
        q.append(plane.gather_queries(queries.reshape(GROUPS, -1, HEAD_DIM, LANES)))

    def merged(merge):
        out, low = next(merge)
        kept.append(out)
        attended.append(along_g(low))
        return low

    for head in range(GROUP_HEADS):
        for later in {0: (0, 1), 1: (2,)}.get(head, ()):
            fetch(later, [outs[0]] if later > 1 else [])
        for clip in range(clips):
            after = []
            if clip == 0 and head > 0:
                merges.append(plane.merge(outs))
                after = [outs[0]]
                outs = ()
                if head > 1:
                    after.append(merged(merges[-2]))
            if clip == clips - 1:
                if head > 0:
                    after = next(merges[-1])
                if fast and head + 1 < GROUP_HEADS:
                    after += [q[head + 1][1]]
            outs = attend(info, kv[head], q[head], clip, clips, times, frames, plane.parts, outs, after)
    merges.append(plane.merge(outs))
    next(merges[-1])
    for merge in merges[len(attended) :]:
        merged(merge)
    if fast:
        size = moment.shape[0] // LANES
        block_out, back_hidden, early, grad = middle(
            info, x, out_grad.reshape(rows, width), keep_rows, w_proj, proj_bias, norm2_gain, norm2_shift, w_fc1, fc1_bias,
            w_fc2, fc2_bias, attended,
        )
        block_out = block_out.reshape(tokens.shape)
        early_windows = pack_early(devices, size, *early)
    else:
        attended_low = jnp.concatenate(attended, axis=1).reshape(width, rows)
        branch = dot32(attended_low, w_proj, (0, 0)) + proj_bias
        hidden = x.astype(F32) + branch
        normed2, norm2_pull = jax.vjp(layer_norm, hidden, norm2_gain, norm2_shift)
        normed2_low = normed2.astype(BF16)
        preactive = dot32(normed2_low, w_fc1, (1, 0)) + fc1_bias
        activated, gelu_pull = jax.vjp(gelu_exact, preactive)
        activated_low = activated.astype(BF16)
        branch2 = dot32(activated_low, w_fc2, (1, 0)) + fc2_bias
        block_out = ((hidden + branch2) * keep_rows).astype(BF16).reshape(tokens.shape)
        grad_out = out_grad.astype(F32).reshape(rows, width) * keep_rows
        back_branch2 = grad_out.astype(BF16)
        grad_fc2_bias = jnp.sum(back_branch2.astype(F32), axis=0)
        back_activated = dot32(back_branch2, w_fc2, (1, 1))
        back_preactive = gelu_pull(back_activated)[0].astype(BF16)
        grad_fc1_bias = jnp.sum(back_preactive.astype(F32), axis=0)
        back_normed2 = dot32(back_preactive, w_fc1, (1, 1))
        back_hidden_norm, grad_norm2_gain, grad_norm2_shift = norm2_pull(back_normed2)
        back_hidden = grad_out + back_hidden_norm
        back_branch = back_hidden.astype(BF16)
        grad_proj_bias = jnp.sum(back_branch.astype(F32), axis=0)
        back_attended = dot32(w_proj, back_branch, (1, 1)).astype(BF16)
        early_windows = info
        grad = back_attended.reshape(GROUPS, -1, rows)
    ready = grad_rows_of(along_g(grad), kept, early_windows)
    back, outs = [], ()
    for head in range(GROUP_HEADS):
        grads = plane.gather_grads(hold(ready[head], one) if head > 0 else ready[head])
        if fast and head == 0:
            early_sum = hold(early_windows, grads)
            early_sum = lax.psum_scatter(early_sum, ("f", "g") + time_axes, scatter_dimension=0, tiled=False)
        before, outs = outs, ()
        for clip in range(clips):
            after = []
            if head > 0 and clip == 0:
                after = [before[0]]
            elif head > 0:
                after = [plane.sum_back(before)]
                back.append(along_g(after[0]))
            outs = attend_back(info, kv[head], q[head], grads, clip, clips, times, frames, plane.parts, outs, after)
            one = [outs[0]] if clip == 0 else one
    back.append(along_g(plane.sum_back(outs)))
    if fast:
        input_grad, *late_windows = finish(
            size, info, x, norm1_gain, norm1_shift, w_qkv, back_hidden, back
        )
        input_grad = input_grad.reshape(tokens.shape)
        late_sum = reduce_late(*late_windows)
        weight_grad = own_chunk(lax.optimization_barrier(early_sum.astype(F32)), late_sum, moment.shape[0])
    else:
        back = jnp.stack(back, axis=1)
        back_kv = back[:, :, :rows].transpose(2, 0, 1, 3).reshape(rows, 2 * width)
        back_q = back[:, :, rows:].reshape(GROUPS, GROUP_HEADS, -1, HEAD_DIM, LANES).transpose(0, 1, 3, 2, 4).reshape(width, rows)
        grad_query_bias = jnp.sum(back_q.astype(F32), axis=1)
        grad_kv_bias = jnp.sum(back_kv.astype(F32), axis=0)
        grad_value_bias = grad_kv_bias.reshape(HEADS, 2, HEAD_DIM)[:, 1].reshape(width)
        normed, norm1_pull = jax.vjp(layer_norm, x.astype(F32), norm1_gain, norm1_shift)
        normed_low = normed.astype(BF16)
        head_dims = (width, GROUPS, GROUP_HEADS, HEAD_DIM)
        w_q = w_qkv[:, :width]
        w_kv = [w_qkv[:, width : 2 * width].reshape(head_dims), w_qkv[:, 2 * width :].reshape(head_dims)]
        w_kv = jnp.stack(w_kv, axis=3).reshape(width, 2 * width)
        back_normed = dot32(back_q, w_q, (0, 1)) + dot32(back_kv, w_kv, (1, 1))
        back_input_norm, grad_norm1_gain, grad_norm1_shift = norm1_pull(back_normed)
        input_grad = (back_hidden + back_input_norm).astype(BF16).reshape(tokens.shape)
        grad_proj = dot32(attended_low, back_branch, (1, 0))
        grad_fc1 = dot32(normed2_low, back_preactive, (0, 0))
        grad_fc2 = dot32(activated_low, back_branch2, (0, 0))
        grad_q = dot32(normed_low, back_q, (0, 1))
        grad_kv = dot32(normed_low, back_kv, (0, 0)).reshape(width, HEADS, 2, HEAD_DIM)
        grad_qkv = jnp.concatenate([grad_q, grad_kv[:, :, 0].reshape(width, width), grad_kv[:, :, 1].reshape(width, width)], axis=1)
        joined = jnp.concatenate(
            [
                grad_norm1_gain,
                grad_norm1_shift,
                grad_qkv.reshape(-1),
                grad_query_bias,
                grad_value_bias,
                grad_proj.reshape(-1),
                grad_proj_bias,
                grad_norm2_gain,
                grad_norm2_shift,
                grad_fc1.reshape(-1),
                grad_fc1_bias,
                grad_fc2.reshape(-1),
                grad_fc2_bias,
            ]
        ).astype(BF16)
        padding = moment.shape[0] * devices - joined.shape[0]
        joined = jnp.concatenate([joined, jnp.zeros((padding,), BF16)])
        weight_grad = lax.psum_scatter(joined, ("f", "g") + time_axes, scatter_dimension=0, tiled=True).astype(F32)
    new_moment = ema_decay[0] * moment + (1.0 - ema_decay[0]) * weight_grad
    return (block_out, input_grad, weight_grad, new_moment)


def solution(mesh):
    freqs, times = mesh.shape["freq"], mesh.shape["tm"]
    if (freqs, times) == (2, 16):
        time_sizes, time_axes = (2, 2), ("x", "c")
    else:
        time_sizes, time_axes = (times // GROUPS,), ("t",)
    fine = Mesh(mesh.devices.reshape(freqs, GROUPS, *time_sizes), ("f", "g") + time_axes)
    patches = P(None, "f", ("g",) + time_axes, None)
    flat = P(("f", "g") + time_axes)
    return jax.shard_map(
        functools.partial(per_device, time_axes),
        mesh=fine,
        in_specs=(patches, patches) + (P(),) * 14 + (flat, P()),
        out_specs=(patches, patches, flat, flat),
        check_vma=False,
    )
```

profile of v0, /device:TPU:0, one launch (start us, length us, event | category | flops | bytes accessed | tf_op | source)
XLA Modules:
  0.0 658.5 jit_solution(10158854579512507944)
XLA Ops:
  14.4 6.7 %shard_map.201 = (bf16[4,768,128]{2,1,0:T(8,128)(2,1)}, bf16[4,768,128]{2,1,0:T(8,128)(2,1)}, bf16[4,768,128]{2,1,0:T(8,128)(2,1)}) custom-call(s32[6]{0:T(128)} %stack.27.info_ref, bf16[512,768]{1,0:T(8,128)(2,1)} %bitcast.118, f32[768]{0:T(1024)} %gain_ref.5, f32[768]{0:T(1024)} %shift_ref.5, bf16[768,2304]{1,0:T(8,128)(2,1)} %w_ref.3, ...), custom_call_target="tpu_custom_call" | custom-call | flops 1811939328 | bytes 3623878 | tf_op jit(solution)/shard_map/pallas_call | solution.py:514
  21.1 26.4 %all_to_all.50 = bf16[4,768,128]{2,1,0:T(8,128)(2,1)S(1)} all-to-all(bf16[4,768,128]{2,1,0:T(8,128)(2,1)} %get-tuple-element.76), channel_id=1, replica_groups=mesh['f'=2,'g'=4,'x'=2,'c'=2] {'g'}, dimensions={0} | all-to-all | bytes 1572864 | tf_op jit(solution)/shard_map/all_to_all | solution.py:669
  47.6 3.5 all-to-all-start.1
  54.3 5.1 collective-permute-done.1.refs_3_
  59.4 10.8 %all-to-all-done.1 = bf16[4,768,128]{2,1,0:T(8,128)(2,1)S(1)} async-done(((bf16[4,768,128]{2,1,0:T(8,128)(2,1)}), bf16[4,768,128]{2,1,0:T(8,128)(2,1)S(1)}, u32[]{:S(2)}, u32[]{:S(2)}) %all-to-all-start.1) | async-done | bytes 786464 | tf_op jit(solution)/shard_map/all_to_all | solution.py:669
  72.5 3.5 all-to-all-start.3
  76.8 12.6 %shard_map.202 = (f32[2,4,72,512]{3,2,1,0:T(8,128)}, f32[2,4,72,512]{3,2,1,0:T(8,128)}) custom-call(s32[6]{0:T(128)} %stack.27.info_ref, bf16[1,4,2,256,128]{4,3,2,1,0:T(8,128)(2,1)} %bitcast.93, bf16[1,4,2,256,128]{4,3,2,1,0:T(8,128)(2,1)} %bitcast.129, bf16[4,4,64,128]{3,2,1,0:T(8,128)(2,1)} %bitcast.113, bf16[4,4,64,128]{3,2,1,0:T(8,128)(2,1)} %copy-done.48, ...), custom_call_target="tpu_custom_call" | custom-call | flops 2147483648 | bytes 524288 | tf_op jit(solution)/shard_map/pallas_call | solution.py:140
  90.1 12.6 %shard_map.203 = (f32[2,4,72,512]{3,2,1,0:T(8,128)}, f32[2,4,72,512]{3,2,1,0:T(8,128)}) custom-call(s32[6]{0:T(128)} %stack.27.info_ref, bf16[1,4,2,256,128]{4,3,2,1,0:T(8,128)(2,1)} %bitcast.94, bf16[1,4,2,256,128]{4,3,2,1,0:T(8,128)(2,1)} %bitcast.130, bf16[4,4,64,128]{3,2,1,0:T(8,128)(2,1)} %bitcast.114, ...), custom_call_target="tpu_custom_call", output_to_operand_aliasing={{0}: (7, {}), {1}: (8, {})} | custom-call | flops 2147483648 | bytes 524288 | tf_op jit(solution)/shard_map/pallas_call | solution.py:140
  106.9 11.3 %collective-permute-done.7 = bf16[4,2,256,128]{3,2,1,0:T(8,128)(2,1)S(1)} collective-permute-done((bf16[4,2,256,128]{3,2,1,0:T(8,128)(2,1)}, bf16[4,2,256,128]{3,2,1,0:T(8,128)(2,1)S(1)}, u32[]{:S(2)}, u32[]{:S(2)}) %collective-permute-start.7) | collective-permute-done | bytes 524320 | tf_op jit(solution)/shard_map/ppermute | solution.py:428
  119.1 12.7 %shard_map.206 = (f32[2,4,72,512]{3,2,1,0:T(8,128)}, f32[2,4,72,512]{3,2,1,0:T(8,128)}) custom-call(s32[6]{0:T(128)} %stack.27.info_ref, bf16[1,4,2,256,128]{4,3,2,1,0:T(8,128)(2,1)} %bitcast.15.refs_0_, bf16[1,4,2,256,128]{4,3,2,1,0:T(8,128)(2,1)} %bitcast.125, bf16[4,4,64,128]{3,2,1,0:T(8,128)(2,1)} %bitcast.14.refs_2_, ...), custom_call_target="tpu_custom_call" | custom-call | flops 2147483648 | bytes 524288 | tf_op jit(solution)/shard_map/pallas_call | solution.py:140
  132.8 2.8 shard_map.204
  136.3 12.7 %shard_map.207 = (f32[2,4,72,512]{3,2,1,0:T(8,128)}, f32[2,4,72,512]{3,2,1,0:T(8,128)}) custom-call(s32[6]{0:T(128)} %stack.27.info_ref, bf16[1,4,2,256,128]{4,3,2,1,0:T(8,128)(2,1)} %bitcast.15.refs_0_, bf16[1,4,2,256,128]{4,3,2,1,0:T(8,128)(2,1)} %bitcast.126, ...), custom_call_target="tpu_custom_call", output_to_operand_aliasing={{0}: (7, {}), {1}: (8, {})} | custom-call | flops 2147483648 | bytes 524288 | tf_op jit(solution)/shard_map/pallas_call | solution.py:140
  152.5 7.9 %collective-permute-done.6.came_ref = bf16[4,80,512]{2,1,0:T(8,128)(2,1)S(1)} collective-permute-done((bf16[4,80,512]{2,1,0:T(8,128)(2,1)S(1)}, bf16[4,80,512]{2,1,0:T(8,128)(2,1)S(1)}, u32[]{:S(2)}, u32[]{:S(2)}) %collective-permute-start.6) | collective-permute-done | bytes 327712 | tf_op jit(solution)/shard_map/ppermute | solution.py:428
  164.3 12.6 %shard_map.210 = (f32[2,4,72,512]{3,2,1,0:T(8,128)}, f32[2,4,72,512]{3,2,1,0:T(8,128)}) custom-call(s32[6]{0:T(128)} %stack.27.info_ref, bf16[1,4,2,256,128]{4,3,2,1,0:T(8,128)(2,1)} %bitcast.88, bf16[1,4,2,256,128]{4,3,2,1,0:T(8,128)(2,1)} %bitcast.121, bf16[4,4,64,128]{3,2,1,0:T(8,128)(2,1)} %bitcast.107, bf16[4,4,64,128]{3,2,1,0:T(8,128)(2,1)} %copy-done.42, ...), custom_call_target="tpu_custom_call" | custom-call | flops 2147483648 | bytes 524288 | tf_op jit(solution)/shard_map/pallas_call | solution.py:140
  177.9 2.8 shard_map.208
  180.7 12.8 %shard_map.211 = (f32[2,4,72,512]{3,2,1,0:T(8,128)}, f32[2,4,72,512]{3,2,1,0:T(8,128)}) custom-call(s32[6]{0:T(128)} %stack.27.info_ref, bf16[1,4,2,256,128]{4,3,2,1,0:T(8,128)(2,1)} %bitcast.89, bf16[1,4,2,256,128]{4,3,2,1,0:T(8,128)(2,1)} %bitcast.122, bf16[4,4,64,128]{3,2,1,0:T(8,128)(2,1)} %bitcast.108, ...), custom_call_target="tpu_custom_call", output_to_operand_aliasing={{0}: (7, {}), {1}: (8, {})} | custom-call | flops 2147483648 | bytes 524288 | tf_op jit(solution)/shard_map/pallas_call | solution.py:140
  193.4 5.1 all-to-all-start.2
  200.5 7.9 %collective-permute-done.12.came_ref = bf16[4,80,512]{2,1,0:T(8,128)(2,1)S(1)} collective-permute-done((bf16[4,80,512]{2,1,0:T(8,128)(2,1)S(1)}, bf16[4,80,512]{2,1,0:T(8,128)(2,1)S(1)}, u32[]{:S(2)}, u32[]{:S(2)}) %collective-permute-start.12) | collective-permute-done | bytes 327712 | tf_op jit(solution)/shard_map/ppermute | solution.py:428
  211.3 4.8 all-to-all-start.4
  217.1 2.8 shard_map.212
  221.4 7.2 %collective-permute-done.17.came_ref = bf16[4,80,512]{2,1,0:T(8,128)(2,1)S(1)} collective-permute-done((bf16[4,80,512]{2,1,0:T(8,128)(2,1)}, bf16[4,80,512]{2,1,0:T(8,128)(2,1)S(1)}, u32[]{:S(2)}, u32[]{:S(2)}) %collective-permute-start.17) | collective-permute-done | bytes 327712 | tf_op jit(solution)/shard_map/ppermute | solution.py:428
  231.5 5.0 all-to-all-start.5
  237.5 5.6 all-to-all-done.5.refs_2_
  243.8 23.4 %shard_map.214 = (bf16[512,768]{1,0:T(8,128)(2,1)}, f32[512,768]{1,0:T(8,128)}, bf16[768,512]{1,0:T(8,128)(2,1)}, bf16[512,768]{1,0:T(8,128)(2,1)}, bf16[512,768...) custom-call(s32[6]{0:T(128)} %stack.27.info_ref, ...), custom_call_target="tpu_custom_call" | custom-call | flops 10871635968 | bytes 21743272 | tf_op jit(solution)/shard_map/pallas_call | solution.py:514
  267.2 3.5 all-to-all-start.6
  270.8 26.1 %shard_map.215.refs_3_ = bf16[32,1744,128]{2,1,0:T(8,128)(2,1)} custom-call(bf16[768,512]{1,0:T(8,128)(2,1)} %get-tuple-element.108.att_ref, bf16[512,768]{1,0:T(8,128)(2,1)} %get-tuple-element.109.branch_ref, bf16[512,768]{1,0:T(8,128)(2,1)} %get-tuple-element.110.normed_ref, bf16[512,3072]{1,0:T(8,128)(2,1)} %get-tuple-element.111.pre_ref, ...), custom_call_target="tpu_custom_call" | custom-call | flops 5445255168 | bytes 21270528 | tf_op jit(solution)/shard_map/pallas_call | solution.py:412
  297.8 2.8 shard_map.216
  301.4 6.4 collective-permute-done.18.refs_7_
  310.2 26.5 %shard_map.217 = (bf16[2,4,64,512]{3,2,1,0:T(8,128)(2,1)}, bf16[2,4,64,512]{3,2,1,0:T(8,128)(2,1)}, bf16[1,4,2,256,128]{4,3,2,1,0:T(8,128)(2,1)}, bf16[1,4,2,256,128]{4,3,2,1,0:T(8,128)(2,1)}) custom-call(s32[6]{0:T(128)} %stack.27.info_ref, bf16[1,4,2,256,128]{4,3,2,1,0:T(8,128)(2,1)} %bitcast.95, bf16[1,4,2,256,128]{4,3,2,1,0:T(8,128)(2,1)} %bitcast.131, ...), custom_call_target="tpu_custom_call" | custom-call | flops 5368709120 | bytes 1048576 | tf_op jit(solution)/shard_map/pallas_call | solution.py:235
  336.7 26.8 %shard_map.218 = (bf16[2,4,64,512]{3,2,1,0:T(8,128)(2,1)}, bf16[2,4,64,512]{3,2,1,0:T(8,128)(2,1)}, bf16[1,4,2,256,128]{4,3,2,1,0:T(8,128)(2,1)}, bf16[1,4,2,256,128]{4,3,2,1,0:T(8,128)(2,1)}) custom-call(s32[6]{0:T(128)} %stack.27.info_ref, ...), custom_call_target="tpu_custom_call", output_to_operand_aliasing={{0}: (11, {}), {1}: (12, {}), {2}: (13, {}), {3}: (14, {})} | custom-call | flops 5368709120 | bytes 1048576 | tf_op jit(solution)/shard_map/pallas_call | solution.py:235
  366.2 16.0 %collective-permute-done.24.refs_7_ = bf16[4,80,512]{2,1,0:T(8,128)(2,1)S(1)} collective-permute-done((bf16[4,80,512]{2,1,0:T(8,128)(2,1)S(1)}, bf16[4,80,512]{2,1,0:T(8,128)(2,1)S(1)}, u32[]{:S(2)}, u32[]{:S(2)}) %collective-permute-start.24) | collective-permute-done | bytes 327712 | tf_op jit(solution)/shard_map/ppermute | solution.py:428
  386.2 26.5 %shard_map.220 = (bf16[2,4,64,512]{3,2,1,0:T(8,128)(2,1)}, bf16[2,4,64,512]{3,2,1,0:T(8,128)(2,1)}, bf16[1,4,2,256,128]{4,3,2,1,0:T(8,128)(2,1)}, bf16[1,4,2,256,128]{4,3,2,1,0:T(8,128)(2,1)}) custom-call(s32[6]{0:T(128)} %stack.27.info_ref, bf16[1,4,2,256,128]{4,3,2,1,0:T(8,128)(2,1)} %bitcast.15.refs_0_, bf16[1,4,2,256,128]{4,3,2,1,0:T(8,128)(2,1)} %bitcast.127, ...), custom_call_target="tpu_custom_call" | custom-call | flops 5368709120 | bytes 1048576 | tf_op jit(solution)/shard_map/pallas_call | solution.py:235
  416.0 26.6 %shard_map.221 = (bf16[2,4,64,512]{3,2,1,0:T(8,128)(2,1)}, bf16[2,4,64,512]{3,2,1,0:T(8,128)(2,1)}, bf16[1,4,2,256,128]{4,3,2,1,0:T(8,128)(2,1)}, bf16[1,4,2,256,128]{4,3,2,1,0:T(8,128)(2,1)}) custom-call(s32[6]{0:T(128)} %stack.27.info_ref, ...), custom_call_target="tpu_custom_call", output_to_operand_aliasing={{0}: (11, {}), {1}: (12, {}), {2}: (13, {}), {3}: (14, {})} | custom-call | flops 5368709120 | bytes 1048576 | tf_op jit(solution)/shard_map/pallas_call | solution.py:235
  444.6 6.5 all-to-all-start.7
  451.3 11.9 %collective-permute-done.30.refs_7_ = bf16[4,80,512]{2,1,0:T(8,128)(2,1)S(1)} collective-permute-done((bf16[4,80,512]{2,1,0:T(8,128)(2,1)S(1)}, bf16[4,80,512]{2,1,0:T(8,128)(2,1)S(1)}, u32[]{:S(2)}, u32[]{:S(2)}) %collective-permute-start.30) | collective-permute-done | bytes 327712 | tf_op jit(solution)/shard_map/ppermute | solution.py:428
  465.7 26.8 %shard_map.223 = (bf16[2,4,64,512]{3,2,1,0:T(8,128)(2,1)}, bf16[2,4,64,512]{3,2,1,0:T(8,128)(2,1)}, bf16[1,4,2,256,128]{4,3,2,1,0:T(8,128)(2,1)}, bf16[1,4,2,256,128]{4,3,2,1,0:T(8,128)(2,1)}) custom-call(s32[6]{0:T(128)} %stack.27.info_ref, bf16[1,4,2,256,128]{4,3,2,1,0:T(8,128)(2,1)} %bitcast.90, bf16[1,4,2,256,128]{4,3,2,1,0:T(8,128)(2,1)} %bitcast.123, ...), custom_call_target="tpu_custom_call" | custom-call | flops 5368709120 | bytes 1048576 | tf_op jit(solution)/shard_map/pallas_call | solution.py:235
  495.8 26.5 %shard_map.224 = (bf16[2,4,64,512]{3,2,1,0:T(8,128)(2,1)}, bf16[2,4,64,512]{3,2,1,0:T(8,128)(2,1)}, bf16[1,4,2,256,128]{4,3,2,1,0:T(8,128)(2,1)}, bf16[1,4,2,256,128]{4,3,2,1,0:T(8,128)(2,1)}) custom-call(s32[6]{0:T(128)} %stack.27.info_ref, ...), custom_call_target="tpu_custom_call", output_to_operand_aliasing={{0}: (11, {}), {1}: (12, {}), {2}: (13, {}), {3}: (14, {})} | custom-call | flops 5368709120 | bytes 1048576 | tf_op jit(solution)/shard_map/pallas_call | solution.py:235
  522.7 6.2 all-to-all-start.8
  531.1 11.9 %collective-permute-done.33 = bf16[4,2,256,128]{3,2,1,0:T(8,128)(2,1)S(1)} collective-permute-done((bf16[4,2,256,128]{3,2,1,0:T(8,128)(2,1)}, bf16[4,2,256,128]{3,2,1,0:T(8,128)(2,1)S(1)}, u32[]{:S(2)}, u32[]{:S(2)}) %collective-permute-start.33) | collective-permute-done | bytes 524320 | tf_op jit(solution)/shard_map/ppermute | solution.py:428
  546.3 3.2 all-to-all-done.8.refs_1_
  549.5 24.3 %all_to_all.51.refs_2_ = bf16[4,768,128]{2,1,0:T(8,128)(2,1)} all-to-all(bf16[4,768,128]{2,1,0:T(8,128)(2,1)} %shard_map.225), channel_id=1, replica_groups=mesh['f'=2,'g'=4,'x'=2,'c'=2] {'g'}, dimensions={0} | all-to-all | bytes 1572864 | tf_op jit(solution)/shard_map/all_to_all | solution.py:669
  573.8 13.3 %shard_map.226 = (bf16[512,768]{1,0:T(8,128)(2,1)}, bf16[4,1792,128]{2,1,0:T(8,128)(2,1)}, bf16[4,1792,128]{2,1,0:T(8,128)(2,1)}) custom-call(s32[6]{0:T(128)} %stack.27.info_ref, bf16[512,768]{1,0:T(8,128)(2,1)} %bitcast.120, f32[768]{0:T(1024)} %gain_ref.5, f32[768]{0:T(1024)} %shift_ref.5, bf16[768,2304]{1,0:T(8,128)(2,1)} %w_ref.3, ...), custom_call_target="tpu_custom_call" | custom-call | flops 3623878656 | bytes 7247757 | tf_op jit(solution)/shard_map/pallas_call | solution.py:514
  587.1 4.0 collective-permute-done.36
  595.1 10.9 %collective-permute-done.39 = bf16[2,2,448,128]{3,2,0,1:T(8,128)(2,1)S(1)} collective-permute-done((bf16[2,2,448,128]{3,2,0,1:T(8,128)(2,1)S(1)}, bf16[2,2,448,128]{3,2,0,1:T(8,128)(2,1)S(1)}, u32[]{:S(2)}, u32[]{:S(2)}) %collective-permute-start.39) | collective-permute-done | bytes 458784 | tf_op jit(solution)/shard_map/ppermute | solution.py:428
  608.1 4.9 collective-permute-done.40
  615.6 22.9 %collective-permute-start.43 = (bf16[896,128]{1,0:T(8,128)(2,1)S(1)}, bf16[896,128]{1,0:T(8,128)(2,1)S(1)}, u32[]{:S(2)}, u32[]{:S(2)}) collective-permute-start(bf16[896,128]{1,0:T(8,128)(2,1)S(1)} %dynamic-slice_bitcast_fusion), channel_id=1, source_target_pairs={{0,4},{4,0},{1,5},{5,1},{2,6},{6,2},{3,7},{7,3},{16,20},{20,16},{1... | collective-permute-start | bytes 688136 | tf_op jit(solution)/shard_map/ppermute | solution.py:458
  639.2 3.3 collective-permute-done.43
  643.5 5.1 collective-permute-done.44
  (225 shorter events, 76.1 us)
Async XLA Ops:
  47.6 22.7 %all-to-all-start.1 = ((bf16[4,768,128]{2,1,0:T(8,128)(2,1)}), bf16[4,768,128]{2,1,0:T(8,128)(2,1)S(1)}, u32[]{:S(2)}, u32[]{:S(2)}) async-start(bf16[4,768,128]{2,1,0:T(8,128)(2,1)} %get-tuple-element.79), calls=%async_computation.1 | async-start | bytes 1572864 | tf_op jit(solution)/shard_map/all_to_all | solution.py:669
  51.1 24.9 %collective-permute-start = (bf16[4,2,256,128]{3,2,1,0:T(8,128)(2,1)S(1)}, bf16[4,2,256,128]{3,2,1,0:T(8,128)(2,1)S(1)}, u32[]{:S(2)}, u32[]{:S(2)}) collective-permute-start(bf16[4,2,256,128]{3,2,1,0:T(8,128)(2,1)S(1)} %bitcast.92), channel_id=1, source_target_pairs={{0,16},{16,0},{1,17},{17,1},{2,18},{18,2},{3,19},{19,3},{4,20},{20... | collective-permute-start | bytes 1572872 | tf_op jit(solution)/shard_map/ppermute | solution.py:428
  52.7 6.7 %collective-permute-start.1 = (bf16[4,4,64,128]{3,2,1,0:T(8,128)(2,1)S(1)}, bf16[4,4,64,128]{3,2,1,0:T(8,128)(2,1)S(1)}, u32[]{:S(2)}, u32[]{:S(2)}) collective-permute-start(bf16[4,4,64,128]{3,2,1,0:T(8,128)(2,1)S(1)} %bitcast.111), channel_id=1, source_target_pairs={{0,2},{2,0},{1,3},{3,1},{4,6},{6,4},{5,7},{7,5},{8,10},{10,8},{9,1... | collective-permute-start | bytes 786440 | tf_op jit(solution)/shard_map/ppermute | solution.py:428
  54.3 21.7 %collective-permute-start.2 = (bf16[4,4,64,128]{3,2,1,0:T(8,128)(2,1)S(1)}, bf16[4,4,64,128]{3,2,1,0:T(8,128)(2,1)}, u32[]{:S(2)}, u32[]{:S(2)}) collective-permute-start(bf16[4,4,64,128]{3,2,1,0:T(8,128)(2,1)S(1)} %bitcast.112), channel_id=1, source_target_pairs={{0,1},{1,0},{2,3},{3,2},{4,5},{5,4},{6,7},{7,6},{8,9},{9,8},{10,11... | collective-permute-start | bytes 786440 | tf_op jit(solution)/shard_map/ppermute | solution.py:428
  59.4 16.6 %collective-permute-start.3 = (bf16[4,4,64,128]{3,2,1,0:T(8,128)(2,1)S(1)}, bf16[4,4,64,128]{3,2,1,0:T(8,128)(2,1)}, u32[]{:S(2)}, u32[]{:S(2)}) collective-permute-start(bf16[4,4,64,128]{3,2,1,0:T(8,128)(2,1)S(1)} %collective-permute-done.1.refs_3_), channel_id=1, source_target_pairs={{0,1},{1,0},{2,3},{3,2},{4,5},{5,4},{6,7},{7,6},{8,9},{9,8},{10,11... | collective-permute-start | bytes 786440 | tf_op jit(solution)/shard_map/ppermute | solution.py:428
  71.0 18.4 %collective-permute-start.4 = (bf16[4,4,64,128]{3,2,1,0:T(8,128)(2,1)}, bf16[4,4,64,128]{3,2,1,0:T(8,128)(2,1)S(1)}, u32[]{:S(2)}, u32[]{:S(2)}) collective-permute-start(bf16[4,4,64,128]{3,2,1,0:T(8,128)(2,1)} %bitcast.14.refs_2_), channel_id=1, source_target_pairs={{0,2},{2,0},{1,3},{3,1},{4,6},{6,4},{5,7},{7,5},{8,10},{10,8},{9,1... | collective-permute-start | bytes 786440 | tf_op jit(solution)/shard_map/ppermute | solution.py:428
  72.5 33.2 %all-to-all-start.3 = ((bf16[4,768,128]{2,1,0:T(8,128)(2,1)}), bf16[4,768,128]{2,1,0:T(8,128)(2,1)S(1)}, u32[]{:S(2)}, u32[]{:S(2)}) async-start(bf16[4,768,128]{2,1,0:T(8,128)(2,1)} %get-tuple-element.87), calls=%async_computation.3 | async-start | bytes 1572864 | tf_op jit(solution)/shard_map/all_to_all | solution.py:669
  102.8 29.0 %collective-permute-start.5 = (f32[2,4,72,512]{3,2,1,0:T(8,128)}, f32[2,4,72,512]{3,2,1,0:T(8,128)S(1)}, u32[]{:S(2)}, u32[]{:S(2)}) collective-permute-start(f32[2,4,72,512]{3,2,1,0:T(8,128)} %get-tuple-element.81), channel_id=1, source_target_pairs={{0,1},{1,0},{2,3},{3,2},{4,5},{5,4},{6,7},{7,6},{8,9},{9,8},{10,11... | collective-permute-start | bytes 3538952 | tf_op jit(solution)/shard_map/ppermute | solution.py:428
  103.6 14.5 %collective-permute-start.7 = (bf16[4,2,256,128]{3,2,1,0:T(8,128)(2,1)}, bf16[4,2,256,128]{3,2,1,0:T(8,128)(2,1)S(1)}, u32[]{:S(2)}, u32[]{:S(2)}) collective-permute-start(bf16[4,2,256,128]{3,2,1,0:T(8,128)(2,1)} %bitcast.16), channel_id=1, source_target_pairs={{0,16},{16,0},{1,17},{17,1},{2,18},{18,2},{3,19},{19,3},{4,20},{20... | collective-permute-start | bytes 1572872 | tf_op jit(solution)/shard_map/ppermute | solution.py:428
  105.4 12.8 %collective-permute-start.9 = (bf16[4,4,64,128]{3,2,1,0:T(8,128)(2,1)}, bf16[4,4,64,128]{3,2,1,0:T(8,128)(2,1)S(1)}, u32[]{:S(2)}, u32[]{:S(2)}) collective-permute-start(bf16[4,4,64,128]{3,2,1,0:T(8,128)(2,1)} %copy-done.43), channel_id=1, source_target_pairs={{0,1},{1,0},{2,3},{3,2},{4,5},{5,4},{6,7},{7,6},{8,9},{9,8},{10,11... | collective-permute-start | bytes 786440 | tf_op jit(solution)/shard_map/ppermute | solution.py:428
  105.7 29.8 %collective-permute-start.10 = (bf16[4,4,64,128]{3,2,1,0:T(8,128)(2,1)S(1)}, bf16[4,4,64,128]{3,2,1,0:T(8,128)(2,1)S(1)}, u32[]{:S(2)}, u32[]{:S(2)}) collective-permute-start(bf16[4,4,64,128]{3,2,1,0:T(8,128)(2,1)S(1)} %bitcast.105), channel_id=1, source_target_pairs={{0,2},{2,0},{1,3},{3,1},{4,6},{6,4},{5,7},{7,5},{8,10},{10,8},{9,1... | collective-permute-start | bytes 786440 | tf_op jit(solution)/shard_map/ppermute | solution.py:428
  149.0 27.9 %collective-permute-start.11 = (f32[2,4,72,512]{3,2,1,0:T(8,128)}, f32[2,4,72,512]{3,2,1,0:T(8,128)S(1)}, u32[]{:S(2)}, u32[]{:S(2)}) collective-permute-start(f32[2,4,72,512]{3,2,1,0:T(8,128)} %get-tuple-element.90), channel_id=1, source_target_pairs={{0,1},{1,0},{2,3},{3,2},{4,5},{5,4},{6,7},{7,6},{8,9},{9,8},{10,11... | collective-permute-start | bytes 3538952 | tf_op jit(solution)/shard_map/ppermute | solution.py:428
  149.0 14.3 %collective-permute-start.13 = (bf16[4,2,256,128]{3,2,1,0:T(8,128)(2,1)S(1)}, bf16[4,2,256,128]{3,2,1,0:T(8,128)(2,1)S(1)}, u32[]{:S(2)}, u32[]{:S(2)}) collective-permute-start(bf16[4,2,256,128]{3,2,1,0:T(8,128)(2,1)S(1)} %bitcast.87), channel_id=1, source_target_pairs={{0,16},{16,0},{1,17},{17,1},{2,18},{18,2},{3,19},{19,3},{4,20},{20... | collective-permute-start | bytes 1572872 | tf_op jit(solution)/shard_map/ppermute | solution.py:428
  150.6 9.8 %collective-permute-start.6 = (bf16[4,80,512]{2,1,0:T(8,128)(2,1)S(1)}, bf16[4,80,512]{2,1,0:T(8,128)(2,1)S(1)}, u32[]{:S(2)}, u32[]{:S(2)}) collective-permute-start(bf16[4,80,512]{2,1,0:T(8,128)(2,1)S(1)} %copy-done.39), channel_id=1, source_target_pairs={{0,2},{2,0},{1,3},{3,1},{4,6},{6,4},{5,7},{7,5},{8,10},{10,8},{9,1... | collective-permute-start | bytes 983048 | tf_op jit(solution)/shard_map/ppermute | solution.py:428
  151.9 11.3 %collective-permute-start.14 = (bf16[4,4,64,128]{3,2,1,0:T(8,128)(2,1)S(1)}, bf16[4,4,64,128]{3,2,1,0:T(8,128)(2,1)S(1)}, u32[]{:S(2)}, u32[]{:S(2)}) collective-permute-start(bf16[4,4,64,128]{3,2,1,0:T(8,128)(2,1)S(1)} %bitcast.106), channel_id=1, source_target_pairs={{0,1},{1,0},{2,3},{3,2},{4,5},{5,4},{6,7},{7,6},{8,9},{9,8},{10,11... | collective-permute-start | bytes 786440 | tf_op jit(solution)/shard_map/ppermute | solution.py:428
  151.9 11.3 %collective-permute-start.15 = (bf16[4,4,64,128]{3,2,1,0:T(8,128)(2,1)}, bf16[4,4,64,128]{3,2,1,0:T(8,128)(2,1)S(1)}, u32[]{:S(2)}, u32[]{:S(2)}) collective-permute-start(bf16[4,4,64,128]{3,2,1,0:T(8,128)(2,1)} %copy-done.42), channel_id=1, source_target_pairs={{0,1},{1,0},{2,3},{3,2},{4,5},{5,4},{6,7},{7,6},{8,9},{9,8},{10,11... | collective-permute-start | bytes 786440 | tf_op jit(solution)/shard_map/ppermute | solution.py:428
  193.4 22.7 %collective-permute-start.16 = (f32[2,4,72,512]{3,2,1,0:T(8,128)}, f32[2,4,72,512]{3,2,1,0:T(8,128)S(1)}, u32[]{:S(2)}, u32[]{:S(2)}) collective-permute-start(f32[2,4,72,512]{3,2,1,0:T(8,128)} %get-tuple-element.98), channel_id=1, source_target_pairs={{0,1},{1,0},{2,3},{3,2},{4,5},{5,4},{6,7},{7,6},{8,9},{9,8},{10,11... | collective-permute-start | bytes 3538952 | tf_op jit(solution)/shard_map/ppermute | solution.py:428
  193.4 17.8 %all-to-all-start.2 = ((bf16[4,64,512]{2,1,0:T(8,128)(2,1)}), bf16[4,64,512]{2,1,0:T(8,128)(2,1)S(1)}, u32[]{:S(2)}, u32[]{:S(2)}) async-start(bf16[4,64,512]{2,1,0:T(8,128)(2,1)} %get-tuple-element.84.refs_7_), calls=%async_computation.2 | async-start | bytes 524288 | tf_op jit(solution)/shard_map/all_to_all | solution.py:669
  198.5 9.8 %collective-permute-start.12 = (bf16[4,80,512]{2,1,0:T(8,128)(2,1)S(1)}, bf16[4,80,512]{2,1,0:T(8,128)(2,1)S(1)}, u32[]{:S(2)}, u32[]{:S(2)}) collective-permute-start(bf16[4,80,512]{2,1,0:T(8,128)(2,1)S(1)} %copy-done.41), channel_id=1, source_target_pairs={{0,2},{2,0},{1,3},{3,1},{4,6},{6,4},{5,7},{7,5},{8,10},{10,8},{9,1... | collective-permute-start | bytes 983048 | tf_op jit(solution)/shard_map/ppermute | solution.py:428
  211.3 20.2 %all-to-all-start.4 = ((bf16[4,64,512]{2,1,0:T(8,128)(2,1)}), bf16[4,64,512]{2,1,0:T(8,128)(2,1)S(1)}, u32[]{:S(2)}, u32[]{:S(2)}) async-start(bf16[4,64,512]{2,1,0:T(8,128)(2,1)} %get-tuple-element.93), calls=%async_computation.4 | async-start | bytes 524288 | tf_op jit(solution)/shard_map/all_to_all | solution.py:669
  219.9 8.6 %collective-permute-start.17 = (bf16[4,80,512]{2,1,0:T(8,128)(2,1)}, bf16[4,80,512]{2,1,0:T(8,128)(2,1)S(1)}, u32[]{:S(2)}, u32[]{:S(2)}) collective-permute-start(bf16[4,80,512]{2,1,0:T(8,128)(2,1)} %get-tuple-element.100), channel_id=1, source_target_pairs={{0,2},{2,0},{1,3},{3,1},{4,6},{6,4},{5,7},{7,5},{8,10},{10,8},{9,1... | collective-permute-start | bytes 983048 | tf_op jit(solution)/shard_map/ppermute | solution.py:428
  231.5 11.6 %all-to-all-start.5 = ((bf16[4,64,512]{2,1,0:T(8,128)(2,1)}), bf16[4,64,512]{2,1,0:T(8,128)(2,1)S(1)}, u32[]{:S(2)}, u32[]{:S(2)}) async-start(bf16[4,64,512]{2,1,0:T(8,128)(2,1)} %get-tuple-element.101), calls=%async_computation.5 | async-start | bytes 524288 | tf_op jit(solution)/shard_map/all_to_all | solution.py:669
  267.2 29.7 %all-to-all-start.6 = ((bf16[4,192,512]{2,1,0:T(8,128)(2,1)}), bf16[4,192,512]{2,1,0:T(8,128)(2,1)S(1)}, u32[]{:S(2)}, u32[]{:S(2)}) async-start(bf16[4,192,512]{2,1,0:T(8,128)(2,1)} %get-tuple-element.104), calls=%async_computation.6 | async-start | bytes 1572864 | tf_op jit(solution)/shard_map/all_to_all | solution.py:669
  270.7 378.0 %reduce-scatter.2.cloned.1.call-start = ((), (), s32[]{:S(2)}) async-start(), calls=%async_computation.11 | async-start | bytes 14733312 | tf_op jit(solution)/shard_map/reduce_scatter | solution.py:868
  300.5 7.3 %collective-permute-start.18 = (bf16[4,80,512]{2,1,0:T(8,128)(2,1)}, bf16[4,80,512]{2,1,0:T(8,128)(2,1)S(1)}, u32[]{:S(2)}, u32[]{:S(2)}) collective-permute-start(bf16[4,80,512]{2,1,0:T(8,128)(2,1)} %get-tuple-element.115.refs_6_), channel_id=1, source_target_pairs={{0,2},{2,0},{1,3},{3,1},{4,6},{6,4},{5,7},{7,5},{8,10},{10,8},{9,1... | collective-permute-start | bytes 983048 | tf_op jit(solution)/shard_map/ppermute | solution.py:428
  301.4 6.4 collective-permute-start.19
  363.5 18.8 %collective-permute-start.22 = (bf16[2,4,64,512]{3,2,1,0:T(8,128)(2,1)}, bf16[2,4,64,512]{3,2,1,0:T(8,128)(2,1)S(1)}, u32[]{:S(2)}, u32[]{:S(2)}) collective-permute-start(bf16[2,4,64,512]{3,2,1,0:T(8,128)(2,1)} %get-tuple-element.123), channel_id=1, source_target_pairs={{0,1},{1,0},{2,3},{3,2},{4,5},{5,4},{6,7},{7,6},{8,9},{9,8},{10,11... | collective-permute-start | bytes 1572872 | tf_op jit(solution)/shard_map/ppermute | solution.py:428
  363.6 18.6 %collective-permute-start.24 = (bf16[4,80,512]{2,1,0:T(8,128)(2,1)S(1)}, bf16[4,80,512]{2,1,0:T(8,128)(2,1)S(1)}, u32[]{:S(2)}, u32[]{:S(2)}) collective-permute-start(bf16[4,80,512]{2,1,0:T(8,128)(2,1)S(1)} %copy-done.30), channel_id=1, source_target_pairs={{0,2},{2,0},{1,3},{3,1},{4,6},{6,4},{5,7},{7,5},{8,10},{10,8},{9,1... | collective-permute-start | bytes 983048 | tf_op jit(solution)/shard_map/ppermute | solution.py:428
  364.5 20.2 %collective-permute-start.25 = (bf16[4,80,512]{2,1,0:T(8,128)(2,1)S(1)}, bf16[4,80,512]{2,1,0:T(8,128)(2,1)S(1)}, u32[]{:S(2)}, u32[]{:S(2)}) collective-permute-start(bf16[4,80,512]{2,1,0:T(8,128)(2,1)S(1)} %copy-done.30), channel_id=1, source_target_pairs={{0,1},{1,0},{2,3},{3,2},{4,5},{5,4},{6,7},{7,6},{8,9},{9,8},{10,11... | collective-permute-start | bytes 983048 | tf_op jit(solution)/shard_map/ppermute | solution.py:428
  364.6 48.1 %collective-permute-start.21 = (bf16[4,2,256,128]{3,2,1,0:T(8,128)(2,1)}, bf16[4,2,256,128]{3,2,1,0:T(8,128)(2,1)S(1)}, u32[]{:S(2)}, u32[]{:S(2)}) collective-permute-start(bf16[4,2,256,128]{3,2,1,0:T(8,128)(2,1)} %bitcast.135), channel_id=1, source_target_pairs={{0,16},{16,0},{1,17},{17,1},{2,18},{18,2},{3,19},{19,3},{4,20},{20... | collective-permute-start | bytes 1572872 | tf_op jit(solution)/shard_map/ppermute | solution.py:428
  384.3 28.5 %collective-permute-start.23 = (bf16[4,64,512]{2,1,0:T(8,128)(2,1)S(1)}, bf16[4,64,512]{2,1,0:T(8,128)(2,1)S(1)}, u32[]{:S(2)}, u32[]{:S(2)}) collective-permute-start(bf16[4,64,512]{2,1,0:T(8,128)(2,1)S(1)} %get-tuple-element.160), channel_id=1, source_target_pairs={{0,2},{2,0},{1,3},{3,1},{4,6},{6,4},{5,7},{7,5},{8,10},{10,8},{9,1... | collective-permute-start | bytes 786440 | tf_op jit(solution)/shard_map/ppermute | solution.py:428
  442.7 20.6 %collective-permute-start.28 = (bf16[2,4,64,512]{3,2,1,0:T(8,128)(2,1)}, bf16[2,4,64,512]{3,2,1,0:T(8,128)(2,1)S(1)}, u32[]{:S(2)}, u32[]{:S(2)}) collective-permute-start(bf16[2,4,64,512]{3,2,1,0:T(8,128)(2,1)} %get-tuple-element.133), channel_id=1, source_target_pairs={{0,1},{1,0},{2,3},{3,2},{4,5},{5,4},{6,7},{7,6},{8,9},{9,8},{10,11... | collective-permute-start | bytes 1572872 | tf_op jit(solution)/shard_map/ppermute | solution.py:428
  442.8 20.4 %collective-permute-start.30 = (bf16[4,80,512]{2,1,0:T(8,128)(2,1)S(1)}, bf16[4,80,512]{2,1,0:T(8,128)(2,1)S(1)}, u32[]{:S(2)}, u32[]{:S(2)}) collective-permute-start(bf16[4,80,512]{2,1,0:T(8,128)(2,1)S(1)} %copy-done.29), channel_id=1, source_target_pairs={{0,2},{2,0},{1,3},{3,1},{4,6},{6,4},{5,7},{7,5},{8,10},{10,8},{9,1... | collective-permute-start | bytes 983048 | tf_op jit(solution)/shard_map/ppermute | solution.py:428
  444.5 19.8 %collective-permute-start.31 = (bf16[4,80,512]{2,1,0:T(8,128)(2,1)S(1)}, bf16[4,80,512]{2,1,0:T(8,128)(2,1)S(1)}, u32[]{:S(2)}, u32[]{:S(2)}) collective-permute-start(bf16[4,80,512]{2,1,0:T(8,128)(2,1)S(1)} %copy-done.29), channel_id=1, source_target_pairs={{0,1},{1,0},{2,3},{3,2},{4,5},{5,4},{6,7},{7,6},{8,9},{9,8},{10,11... | collective-permute-start | bytes 983048 | tf_op jit(solution)/shard_map/ppermute | solution.py:428
  444.6 78.1 %all-to-all-start.7 = ((bf16[4,768,128]{2,1,0:T(8,128)(2,1)}), bf16[4,768,128]{2,1,0:T(8,128)(2,1)S(1)}, u32[]{:S(2)}, u32[]{:S(2)}) async-start(bf16[4,768,128]{2,1,0:T(8,128)(2,1)} %shard_map.219.refs_14_), calls=%async_computation.7 | async-start | bytes 1572864 | tf_op jit(solution)/shard_map/all_to_all | solution.py:669
  451.1 41.4 %collective-permute-start.27 = (bf16[4,2,256,128]{3,2,1,0:T(8,128)(2,1)}, bf16[4,2,256,128]{3,2,1,0:T(8,128)(2,1)S(1)}, u32[]{:S(2)}, u32[]{:S(2)}) collective-permute-start(bf16[4,2,256,128]{3,2,1,0:T(8,128)(2,1)} %bitcast.133), channel_id=1, source_target_pairs={{0,16},{16,0},{1,17},{17,1},{2,18},{18,2},{3,19},{19,3},{4,20},{20... | collective-permute-start | bytes 1572872 | tf_op jit(solution)/shard_map/ppermute | solution.py:428
  464.2 28.3 %collective-permute-start.29 = (bf16[4,64,512]{2,1,0:T(8,128)(2,1)S(1)}, bf16[4,64,512]{2,1,0:T(8,128)(2,1)S(1)}, u32[]{:S(2)}, u32[]{:S(2)}) collective-permute-start(bf16[4,64,512]{2,1,0:T(8,128)(2,1)S(1)} %get-tuple-element.158), channel_id=1, source_target_pairs={{0,2},{2,0},{1,3},{3,1},{4,6},{6,4},{5,7},{7,5},{8,10},{10,8},{9,1... | collective-permute-start | bytes 786440 | tf_op jit(solution)/shard_map/ppermute | solution.py:428
  522.3 7.7 %collective-permute-start.34 = (bf16[2,4,64,512]{3,2,1,0:T(8,128)(2,1)}, bf16[2,4,64,512]{3,2,1,0:T(8,128)(2,1)S(1)}, u32[]{:S(2)}, u32[]{:S(2)}) collective-permute-start(bf16[2,4,64,512]{3,2,1,0:T(8,128)(2,1)} %get-tuple-element.143), channel_id=1, source_target_pairs={{0,1},{1,0},{2,3},{3,2},{4,5},{5,4},{6,7},{7,6},{8,9},{9,8},{10,11... | collective-permute-start | bytes 1572872 | tf_op jit(solution)/shard_map/ppermute | solution.py:428
  522.7 26.8 %all-to-all-start.8 = ((bf16[4,768,128]{2,1,0:T(8,128)(2,1)}), bf16[4,768,128]{2,1,0:T(8,128)(2,1)S(1)}, u32[]{:S(2)}, u32[]{:S(2)}) async-start(bf16[4,768,128]{2,1,0:T(8,128)(2,1)} %shard_map.222.refs_14_), calls=%async_computation.8 | async-start | bytes 1572864 | tf_op jit(solution)/shard_map/all_to_all | solution.py:669
  528.9 14.1 %collective-permute-start.33 = (bf16[4,2,256,128]{3,2,1,0:T(8,128)(2,1)}, bf16[4,2,256,128]{3,2,1,0:T(8,128)(2,1)S(1)}, u32[]{:S(2)}, u32[]{:S(2)}) collective-permute-start(bf16[4,2,256,128]{3,2,1,0:T(8,128)(2,1)} %bitcast.134), channel_id=1, source_target_pairs={{0,16},{16,0},{1,17},{17,1},{2,18},{18,2},{3,19},{19,3},{4,20},{20... | collective-permute-start | bytes 1572872 | tf_op jit(solution)/shard_map/ppermute | solution.py:428
  531.0 12.0 %collective-permute-start.35 = (bf16[4,64,512]{2,1,0:T(8,128)(2,1)S(1)}, bf16[4,64,512]{2,1,0:T(8,128)(2,1)S(1)}, u32[]{:S(2)}, u32[]{:S(2)}) collective-permute-start(bf16[4,64,512]{2,1,0:T(8,128)(2,1)S(1)} %get-tuple-element.156), channel_id=1, source_target_pairs={{0,2},{2,0},{1,3},{3,1},{4,6},{6,4},{5,7},{7,5},{8,10},{10,8},{9,1... | collective-permute-start | bytes 786440 | tf_op jit(solution)/shard_map/ppermute | solution.py:428
  587.1 4.0 collective-permute-start.36
  593.3 12.6 %collective-permute-start.39 = (bf16[2,2,448,128]{3,2,0,1:T(8,128)(2,1)S(1)}, bf16[2,2,448,128]{3,2,0,1:T(8,128)(2,1)S(1)}, u32[]{:S(2)}, u32[]{:S(2)}) collective-permute-start(bf16[2,2,448,128]{3,2,0,1:T(8,128)(2,1)S(1)} %bitcast.103), channel_id=1, source_target_pairs={{0,16},{16,0},{1,17},{17,1},{2,18},{18,2},{3,19},{19,3},{4,20},{20... | collective-permute-start | bytes 1376264 | tf_op jit(solution)/shard_map/ppermute | solution.py:428
  594.7 12.3 %collective-permute-start.37 = (bf16[2,2,448,128]{3,2,0,1:T(8,128)(2,1)S(1)}, bf16[2,2,448,128]{3,2,0,1:T(8,128)(2,1)S(1)}, u32[]{:S(2)}, u32[]{:S(2)}) collective-permute-start(bf16[2,2,448,128]{3,2,0,1:T(8,128)(2,1)S(1)} %bitcast.104), channel_id=1, source_target_pairs={{0,2},{2,0},{1,3},{3,1},{4,6},{6,4},{5,7},{7,5},{8,10},{10,8},{9,1... | collective-permute-start | bytes 1376264 | tf_op jit(solution)/shard_map/ppermute | solution.py:428
  606.1 6.9 %collective-permute-start.40 = (bf16[2,448,128]{2,1,0:T(8,128)(2,1)S(1)}, bf16[2,448,128]{2,1,0:T(8,128)(2,1)S(1)}, u32[]{:S(2)}, u32[]{:S(2)}) collective-permute-start(bf16[2,448,128]{2,1,0:T(8,128)(2,1)S(1)} %dynamic-slice_bitcast_fusion.1), channel_id=1, source_target_pairs={{0,2},{2,0},{1,3},{3,1},{4,6},{6,4},{5,7},{7,5},{8,10},{10,8},{9,1... | collective-permute-start | bytes 688136 | tf_op jit(solution)/shard_map/ppermute | solution.py:428
  607.2 6.6 collective-permute-start.38
  615.6 26.8 %collective-permute-start.43 = (bf16[896,128]{1,0:T(8,128)(2,1)S(1)}, bf16[896,128]{1,0:T(8,128)(2,1)S(1)}, u32[]{:S(2)}, u32[]{:S(2)}) collective-permute-start(bf16[896,128]{1,0:T(8,128)(2,1)S(1)} %dynamic-slice_bitcast_fusion), channel_id=1, source_target_pairs={{0,4},{4,0},{1,5},{5,1},{2,6},{6,2},{3,7},{7,3},{16,20},{20,16},{1... | collective-permute-start | bytes 688136 | tf_op jit(solution)/shard_map/ppermute | solution.py:458
  642.6 6.1 collective-permute-start.44
  (55 other events, 436.1 us)
Sparse Core Ops, SparseCore 0:
  309.6 186.5 reduce-scatter.1
where the time goes:
time: 649 us; the launch traced here: 658 us
  Pallas kernels  330 us (51%)
  waiting for transfers between devices  137 us (21%)
  starting transfers between devices  88.9 us (14%)
  blocking collectives  50.7 us (8%)
  local copies, waits for them, and re-layouts  24 us (4%)
  between operations  20.9 us (3%)
  other arithmetic  6.87 us (1%)
    pallas_call x6, Pallas kernels, attend_back(): pl.pallas_call(functools.partial(attend_back_kernel, clip, times, frames,...  160 us
    ppermute x42, waiting for transfers between devices, swap(): return lax.ppermute(values, axis, SWAP)  114 us
    pallas_call x6, Pallas kernels, attend(): pl.pallas_call(functools.partial(attend_kernel, clip, times, frames, len(...  76.1 us
    all_to_all x2, blocking collectives, along_g(): return lax.all_to_all(values, 'g', 0, 0, tiled=True)  50.7 us
    pallas_call x3, Pallas kernels, one_step(): pl.pallas_call(kernel, grid_spec=pltpu.PrefetchScalarGridSpec(num_scalar_...  43.5 us
    all_to_all x8, starting transfers between devices, along_g(): return lax.all_to_all(values, 'g', 0, 0, tiled=True)  38.1 us
    ppermute x42, starting transfers between devices, swap(): return lax.ppermute(values, axis, SWAP)  26.6 us
    pallas_call x1, Pallas kernels, pack_early(): pl.pallas_call(functools.partial(pack_early_kernel, size, LATE_CHUNKS), g...  26.1 us
  transfers between devices with their start and end apart: 54, of which 22 were waited for; matrix products, arithmetic and copies ran while one was open for 1% of the time, Pallas kernels for 41%

commit v1 on v0

--- a/solution.py
+++ b/solution.py
@@ -27,12 +27,16 @@
 F32 = jnp.float32
 
 
+TOKEN = jax.ShapeDtypeStruct((8, LANES), F32)
+TOKEN_SPEC = pl.BlockSpec((8, LANES), lambda i, *_: (0, 0))
+
+
 def dot32(left, right, contract):
     return lax.dot_general(left, right, ((contract[:1], contract[1:]), ((), ())), preferred_element_type=F32)
 
 
-def work(info_ref, clip, times):
-    t, full, rest = info_ref[1], info_ref[2 + 2 * clip], info_ref[3 + 2 * clip]
+def work(info_ref, clip, times, frames):
+    t, full, rest = info_ref[0], info_ref[1 + clip] // frames, info_ref[1 + clip] % frames
     live = full + (rest > 0).astype(jnp.int32)
     query_blocks = (live + times - 1) // times
     key_blocks = jnp.maximum(full - t + times - 1, 0) // times
@@ -51,9 +55,10 @@
 
 def attend_kernel(clip, times, frames, n_kv, n_q, n_out, info_ref, *refs):
     kv_refs, q_refs, refs = refs[:n_kv], refs[n_kv : n_kv + n_q], refs[n_kv + n_q :]
-    refs = refs[-n_out - 5 :]
-    out_refs, (acc, top, q_pad, scores, tops) = refs[:n_out], refs[n_out:]
-    query_blocks, key_blocks, partial, rest = work(info_ref, clip, times)
+    refs = refs[-n_out - 6 :]
+    out_refs, (token_ref, acc, top, q_pad, scores, tops) = refs[:n_out], refs[n_out:]
+    token_ref[...] = jnp.zeros_like(token_ref)
+    query_blocks, key_blocks, partial, rest = work(info_ref, clip, times, frames)
     width = q_refs[0].shape[1] * q_refs[0].shape[3]
     rows = scores.shape[1]
     for late in range(GROUPS):
@@ -114,31 +119,28 @@
         safe = jnp.where(some, norm, 1.0)
         out = acc[late, :HEAD_DIM, :] / safe
         lse = jnp.where(some, top[late] + jnp.log2(safe), NEGATIVE)
-        p = 0
-        for ref in out_refs:
-            for part in range(ref.shape[0]):
-                cols = slice(p * width, (p + 1) * width)
-                ref[part, late, :HEAD_DIM, :] = out[:, cols]
-                ref[part, late, HEAD_DIM:, :] = jnp.broadcast_to(lse[:, cols], (OUT_ROWS - HEAD_DIM, width))
-                p += 1
-
-
-def specs_of(kv, q, clip, clips):
-    kv_specs = [pl.BlockSpec((a.shape[0], GROUPS, 1, *a.shape[3:]), lambda i, *_: (0, 0, clip, 0, 0)) for a in kv]
+        fill = jnp.zeros((GRAD_ROWS - HEAD_DIM - 3, out.shape[1]), F32)
+        full = jnp.concatenate([out, thirds(lse), fill], axis=0).astype(BF16)
+        for p, ref in enumerate(out_refs):
+            ref[late] = full[:, p * width : (p + 1) * width]
+
+
+def specs_of(kv, q, place, places):
+    kv_specs = [pl.BlockSpec((a.shape[0], GROUPS, 1, *a.shape[3:]), lambda i, *_: (0, 0, place, 0, 0)) for a in kv]
     _, tiles, _, lanes = q[0].shape
-    q_specs = [pl.BlockSpec((GROUPS, tiles // clips, HEAD_DIM, lanes), lambda i, *_: (0, clip, 0, 0)) for a in q]
-    return kv_specs, q_specs, tiles * lanes // clips
-
-
-def attend(info, kv, q, clip, clips, times, frames, parts, before, after):
-    kv_specs, q_specs, width = specs_of(kv, q, clip, clips)
+    q_specs = [pl.BlockSpec((GROUPS, tiles // places, HEAD_DIM, lanes), lambda i, *_: (0, place, 0, 0)) for a in q]
+    return kv_specs, q_specs, tiles * lanes // places
+
+
+def attend(info, kv, q, place, clip, clips, times, frames, before, after):
+    kv_specs, q_specs, width = specs_of(kv, q, place, kv[0].shape[2])
     queries = len(q) * width
     rows = sum(a.shape[0] for a in kv) * kv[0].shape[3]
     pairs = GROUPS * rows * GROUPS * queries
-    out_specs = [pl.BlockSpec((n, GROUPS, OUT_ROWS, width), lambda i, *_: (0, 0, 0, clip)) for n in parts]
+    out_specs = [pl.BlockSpec((GROUPS, GRAD_ROWS, width), lambda i, *_: (0, 0, clip))] * len(q) + [TOKEN_SPEC]
     n_in = 1 + len(kv) + len(q)
     return pl.pallas_call(
-        functools.partial(attend_kernel, clip, times, frames, len(kv), len(q), len(parts)),
+        functools.partial(attend_kernel, clip, times, frames, len(kv), len(q), len(q)),
         grid_spec=pltpu.PrefetchScalarGridSpec(
             num_scalar_prefetch=1,
             grid=(1,),
@@ -152,7 +154,7 @@
                 pltpu.VMEM((2, 1, queries), F32),
             ],
         ),
-        out_shape=[jax.ShapeDtypeStruct((n, GROUPS, OUT_ROWS, clips * width), F32) for n in parts],
+        out_shape=[jax.ShapeDtypeStruct((GROUPS, GRAD_ROWS, clips * width), BF16)] * len(q) + [TOKEN],
         input_output_aliases={n_in + i: i for i in range(len(before))},
         compiler_params=pltpu.CompilerParams(vmem_limit_bytes=VMEM_LIMIT),
         cost_estimate=pl.CostEstimate(flops=256 * pairs, bytes_accessed=pairs // 16, transcendentals=pairs),
@@ -161,10 +163,11 @@
 
 def attend_back_kernel(clip, times, frames, cuts, n_kv, n_q, n_out, info_ref, *refs):
     kv_refs, q_refs, grad_refs = refs[:n_kv], refs[n_kv : n_kv + n_q], refs[n_kv + n_q : n_kv + 2 * n_q]
-    refs = refs[-n_out - n_kv - 8 :]
+    refs = refs[-n_out - n_kv - 9 :]
     back_q_refs, back_kv_refs, refs = refs[:n_out], refs[n_out : n_out + n_kv], refs[n_out + n_kv :]
-    back_q, back_kv, q_cols, grad_cols, q_rows, grad_rows, lse, delta = refs
-    query_blocks, key_blocks, partial, rest = work(info_ref, clip, times)
+    refs[0][...] = jnp.zeros_like(refs[0])
+    _, back_q, back_kv, q_cols, grad_cols, q_rows, grad_rows, lse, delta = refs
+    query_blocks, key_blocks, partial, rest = work(info_ref, clip, times, frames)
     width = grad_refs[0].shape[-1]
     part_rows = kv_refs[0].shape[3]
     rows = back_kv.shape[1]
@@ -211,12 +214,8 @@
     is_key = lax.broadcasted_iota(jnp.int32, (1, PAIR), 1) < HEAD_DIM
     factor = jnp.where(is_key, jnp.float32(LN2), jnp.float32(1.0))
     for late in range(GROUPS):
-        p = 0
-        for ref in back_q_refs:
-            for part in range(ref.shape[0]):
-                cols = slice(p * width, (p + 1) * width)
-                ref[part, late] = (back_q[late, :HEAD_DIM, cols] * SCALE).astype(BF16)
-                p += 1
+        for p, ref in enumerate(back_q_refs):
+            ref[late] = (back_q[late, :HEAD_DIM, p * width : (p + 1) * width] * SCALE).astype(BF16)
         p = 0
         for ref in back_kv_refs:
             for f in range(ref.shape[0]):
@@ -224,21 +223,22 @@
                 p += 1
 
 
-def attend_back(info, kv, q, grad, clip, clips, times, frames, parts, before, after):
-    kv_specs, q_specs, width = specs_of(kv, q, clip, clips)
+def attend_back(info, kv, q, grad, place, clip, clips, times, frames, before, after):
+    kv_specs, q_specs, width = specs_of(kv, q, place, kv[0].shape[2])
     queries = len(q) * width
     rows = sum(a.shape[0] for a in kv) * kv[0].shape[3]
     pairs = GROUPS * rows * GROUPS * queries
     grad_specs = [pl.BlockSpec((GROUPS, GRAD_ROWS, width), lambda i, *_: (0, 0, clip)) for a in grad]
-    q_out = [pl.BlockSpec((n, GROUPS, HEAD_DIM, width), lambda i, *_: (0, 0, 0, clip)) for n in parts]
+    q_out = [pl.BlockSpec((GROUPS, HEAD_DIM, width), lambda i, *_: (0, 0, clip))] * len(q)
+    kv_out = [pl.BlockSpec((a.shape[0], GROUPS, 1, *a.shape[3:]), lambda i, *_: (0, 0, clip, 0, 0)) for a in kv]
     n_in = 1 + len(kv) + len(q) + len(grad)
     return pl.pallas_call(
-        functools.partial(attend_back_kernel, clip, times, frames, 2, len(kv), len(q), len(parts)),
+        functools.partial(attend_back_kernel, clip, times, frames, 2, len(kv), len(q), len(q)),
         grid_spec=pltpu.PrefetchScalarGridSpec(
             num_scalar_prefetch=1,
             grid=(1,),
             in_specs=kv_specs + q_specs + grad_specs + [pl.BlockSpec(memory_space=pl.ANY)] * (len(before) + len(after)),
-            out_specs=q_out + kv_specs,
+            out_specs=q_out + kv_out + [TOKEN_SPEC],
             scratch_shapes=[
                 pltpu.VMEM((GROUPS, PAIR, queries), F32),
                 pltpu.VMEM((GROUPS, rows, PAIR), F32),
@@ -250,8 +250,9 @@
                 pltpu.VMEM((GROUPS, 1, queries), F32),
             ],
         ),
-        out_shape=[jax.ShapeDtypeStruct((n, GROUPS, HEAD_DIM, clips * width), BF16) for n in parts]
-        + [jax.ShapeDtypeStruct(a.shape, BF16) for a in kv],
+        out_shape=[jax.ShapeDtypeStruct((GROUPS, HEAD_DIM, clips * width), BF16)] * len(q)
+        + [jax.ShapeDtypeStruct((a.shape[0], GROUPS, clips, *a.shape[3:]), BF16) for a in kv]
+        + [TOKEN],
         input_output_aliases={n_in + i: i for i in range(len(before))},
         compiler_params=pltpu.CompilerParams(vmem_limit_bytes=VMEM_LIMIT),
         cost_estimate=pl.CostEstimate(flops=640 * pairs, bytes_accessed=pairs // 8, transcendentals=pairs),
@@ -264,52 +265,28 @@
     return jnp.concatenate([high, middle, values - high - middle], axis=0)
 
 
-def blend(left, left_lse, right, right_lse):
-    most = jnp.maximum(left_lse, right_lse)
-    left_part, right_part = jnp.exp2(left_lse - most), jnp.exp2(right_lse - most)
-    total = left_part + right_part
-    return (left * left_part + right * right_part) / total, most + jnp.log2(total)
-
-
-def merge_cores_kernel(kept_ref, came_ref, mine_ref, sent_ref):
+def merge_kernel(_, *refs):
+    part_refs, (out_ref, low_ref) = refs[:-2], refs[-2:]
     for n in range(GROUPS):
-        for part in range(2):
-            left, right = kept_ref[part, n], came_ref[part, n]
-            out, lse = blend(left[:HEAD_DIM], left[HEAD_DIM : HEAD_DIM + 1], right[:HEAD_DIM], right[HEAD_DIM : HEAD_DIM + 1])
-            if part == 0:
-                mine_ref[n, :HEAD_DIM] = out
-                mine_ref[n, HEAD_DIM:] = jnp.broadcast_to(lse, (OUT_ROWS - HEAD_DIM, out.shape[1]))
-            else:
-                fill = jnp.zeros((GRAD_ROWS - HEAD_DIM - 3, out.shape[1]), F32)
-                sent_ref[n] = jnp.concatenate([out, thirds(lse), fill], axis=0).astype(BF16)
-
-
-def merge_cores(kept, came):
-    _, _, _, width = kept.shape
-    return pl.pallas_call(
-        merge_cores_kernel,
-        out_shape=[jax.ShapeDtypeStruct((GROUPS, OUT_ROWS, width), F32), jax.ShapeDtypeStruct((GROUPS, GRAD_ROWS, width), BF16)],
-        compiler_params=pltpu.CompilerParams(vmem_limit_bytes=VMEM_LIMIT),
-    )(kept, came)
-
-
-def merge_chips_kernel(mine_ref, came_ref, out_ref, low_ref):
-    for n in range(GROUPS):
-        left, right = mine_ref[n], came_ref[n].astype(F32)
-        right_lse = right[HEAD_DIM : HEAD_DIM + 1] + right[HEAD_DIM + 1 : HEAD_DIM + 2] + right[HEAD_DIM + 2 : HEAD_DIM + 3]
-        out, lse = blend(left[:HEAD_DIM], left[HEAD_DIM : HEAD_DIM + 1], right[:HEAD_DIM], right_lse)
+        parts = [ref[n].astype(F32) for ref in part_refs]
+        lses = [p[HEAD_DIM : HEAD_DIM + 1] + p[HEAD_DIM + 1 : HEAD_DIM + 2] + p[HEAD_DIM + 2 : HEAD_DIM + 3] for p in parts]
+        most = functools.reduce(jnp.maximum, lses)
+        shares = [jnp.exp2(lse - most) for lse in lses]
+        total = sum(shares)
+        out = sum(p[:HEAD_DIM] * share for p, share in zip(parts, shares)) / total
         low_ref[n] = out.astype(BF16)
         out_ref[n, :HEAD_DIM] = out
-        out_ref[n, HEAD_DIM:] = jnp.broadcast_to(lse, (OUT_ROWS - HEAD_DIM, out.shape[1]))
-
-
-def merge_chips(mine, came):
-    _, _, width = mine.shape
+        out_ref[n, HEAD_DIM:] = jnp.broadcast_to(most + jnp.log2(total), (OUT_ROWS - HEAD_DIM, out.shape[1]))
+
+
+def merge(parts, after):
+    _, _, width = parts[0].shape
     return pl.pallas_call(
-        merge_chips_kernel,
-        out_shape=[jax.ShapeDtypeStruct((GROUPS, OUT_ROWS, width), F32)] + [jax.ShapeDtypeStruct((GROUPS, HEAD_DIM, width), BF16)],
+        merge_kernel,
+        in_specs=[pl.BlockSpec(memory_space=pl.ANY)] + [pl.BlockSpec(memory_space=pltpu.VMEM)] * len(parts),
+        out_shape=[jax.ShapeDtypeStruct((GROUPS, OUT_ROWS, width), F32), jax.ShapeDtypeStruct((GROUPS, HEAD_DIM, width), BF16)],
         compiler_params=pltpu.CompilerParams(vmem_limit_bytes=VMEM_LIMIT),
-    )(mine, came)
+    )(after, *parts)
 
 
 def grad_rows_kernel(grad_ref, *refs):
@@ -335,23 +312,25 @@
     )(grad, *outs, after)
 
 
-def sum_back_kernel(kept_ref, came_ref, q_kept_ref, q_came_ref, ready_ref):
+def sum_back_kernel(_, kept_ref, came_ref, *refs):
+    q_refs, ready_ref = refs[:-1], refs[-1]
     rows = kept_ref.shape[1]
     for n in range(GROUPS):
         ready_ref[n, :rows] = (kept_ref[n].astype(F32) + came_ref[n].astype(F32)).astype(BF16)
-        query = (q_kept_ref[n].astype(F32) + q_came_ref[n].astype(F32)).astype(BF16)
+        query = sum(ref[n].astype(F32) for ref in q_refs).astype(BF16)
         for j in range(rows // LANES):
             at = rows + j * HEAD_DIM
             ready_ref[n, at : at + HEAD_DIM] = query[:, j * LANES : (j + 1) * LANES]
 
 
-def sum_back(kept, came, q_kept, q_came):
+def sum_back(after, kept, came, queries):
     groups, rows, _ = kept.shape
     return pl.pallas_call(
         sum_back_kernel,
+        in_specs=[pl.BlockSpec(memory_space=pl.ANY)] + [pl.BlockSpec(memory_space=pltpu.VMEM)] * (2 + len(queries)),
         out_shape=jax.ShapeDtypeStruct((groups, rows + rows // LANES * HEAD_DIM, LANES), BF16),
         compiler_params=pltpu.CompilerParams(vmem_limit_bytes=VMEM_LIMIT),
-    )(kept, came, q_kept, q_came)
+    )(after, kept, came, *queries)
 
 
 def spread(lines, at, stride, values):
@@ -405,6 +384,11 @@
         write_window((step - first) * size, lines, window_ref)
 
 
+def early_order(chunk):
+    f, g, x, c = chunk // 16, chunk // 4 % 4, chunk // 2 % 2, chunk % 2
+    return ((c * 2 + x) * 2 + f) * 4 + g
+
+
 def pack_early(devices, size, *operands):
     chunks = devices - LATE_CHUNKS
     whole = [pl.BlockSpec(a.shape, lambda j: (0, 0)) for a in operands]
@@ -413,7 +397,7 @@
         functools.partial(pack_early_kernel, size, LATE_CHUNKS),
         grid=(devices,),
         in_specs=whole,
-        out_specs=pl.BlockSpec((1, EARLY_WINDOW, LANES), lambda j: (j, 0, 0)),
+        out_specs=pl.BlockSpec((1, EARLY_WINDOW, LANES), lambda j: (early_order(j), 0, 0)),
         scratch_shapes=[pltpu.VMEM((-(-(chunks - 1) * size // 8) * 8 + EARLY_WINDOW + 8, LANES), F32)],
         out_shape=jax.ShapeDtypeStruct((devices, EARLY_WINDOW, LANES), BF16),
         compiler_params=pltpu.CompilerParams(vmem_limit_bytes=VMEM_LIMIT),
@@ -443,19 +427,14 @@
 LATE_WINDOW = 1792
 
 
-def reduce_late(send, keep):
-    f, g, x = lax.axis_index("f"), lax.axis_index("g"), lax.axis_index("x")
+def reduce_late(send, keep, after):
+    f, x = lax.axis_index("f"), lax.axis_index("x")
     pairs = add(keep, swap(send, "c")).reshape(2, 2, 4, -1, LANES)
     first = trade(trade(pairs[:, :, :2], 1, x, "x"), 1, f, "f")
     second = trade(trade(pairs[:, :, 2:], 2, f, "f"), 1, x, "x")
-    mine = jnp.concatenate([first, second], axis=1)
-    low = jnp.minimum(g, 1)
-    near = add(mine, lax.ppermute(mine, "g", [(3, 2)]))
-    far = lax.ppermute(near, "g", [(2, 1)])
-    mine = jnp.where(g == 1, add(mine, far), mine)
-    sent = lax.dynamic_index_in_dim(mine, 1 - low, 0, keepdims=False)
-    mine = lax.dynamic_index_in_dim(mine, low, 0, keepdims=False)
-    mine = add(mine, lax.ppermute(sent, "g", SWAP))
+    parts = along_g(hold(jnp.stack([first[0], first[1], second[1], second[0]]), [after]))
+    mine = sum(parts[n].astype(F32) for n in range(GROUPS)).astype(BF16)
+    mine = jnp.concatenate([mine, lax.ppermute(mine, "g", [(2, 1), (3, 0)])], axis=0)
     far = swap(mine, "f")
     part = LATE_WINDOW // 4
     return jnp.concatenate([mine[:part], far[:part], mine[part:], far[part:]], axis=0).astype(F32)
@@ -486,11 +465,12 @@
     return pltpu.roll(values, HEAD_DIM, axis=1)
 
 
-def start_kernel(info_ref, x_ref, gain_ref, shift_ref, w_ref, query_bias_ref, value_bias_ref, *refs):
+def start_kernel(x_ref, gain_ref, shift_ref, w_ref, query_bias_ref, value_bias_ref, *refs):
     rows, width = x_ref.shape
 
     def put(head, values):
-        refs[head % GROUP_HEADS][head // GROUP_HEADS, :rows] = values.astype(BF16)
+        at = max(head % GROUP_HEADS - 1, 0) * rows
+        refs[min(head % GROUP_HEADS, 1)][head // GROUP_HEADS, at : at + rows] = values.astype(BF16)
 
     unit, _ = centre(x_ref[...].astype(F32))
     normed = (unit * row(gain_ref) + row(shift_ref)).astype(BF16)
@@ -505,16 +485,20 @@
     query = query.astype(BF16).T
     for head in range(HEADS):
         part = query[head * HEAD_DIM : (head + 1) * HEAD_DIM]
+        ref = refs[min(head % GROUP_HEADS, 1)]
+        first = ref.shape[1] // (rows + rows // LANES * HEAD_DIM) * rows
+        first += max(head % GROUP_HEADS - 1, 0) * rows // LANES * HEAD_DIM
         for tile in range(rows // LANES):
-            at = rows + tile * HEAD_DIM
-            refs[head % GROUP_HEADS][head // GROUP_HEADS, at : at + HEAD_DIM] = part[:, tile * LANES : (tile + 1) * LANES]
+            at = first + tile * HEAD_DIM
+            ref[head // GROUP_HEADS, at : at + HEAD_DIM] = part[:, tile * LANES : (tile + 1) * LANES]
 
 
 def one_step(kernel, info, operands, shapes, scratch, flops):
+    scalars = [] if info is None else [info]
     return pl.pallas_call(
         kernel,
         grid_spec=pltpu.PrefetchScalarGridSpec(
-            num_scalar_prefetch=1,
+            num_scalar_prefetch=len(scalars),
             grid=(1,),
             in_specs=[pl.BlockSpec(a.shape, lambda i, *_, n=a.ndim: (0,) * n) for a in operands],
             out_specs=[pl.BlockSpec(a.shape, lambda i, *_, n=len(a.shape): (0,) * n) for a in shapes],
@@ -523,18 +507,19 @@
         out_shape=shapes,
         compiler_params=pltpu.CompilerParams(vmem_limit_bytes=VMEM_LIMIT),
         cost_estimate=pl.CostEstimate(flops=flops, bytes_accessed=flops // 500, transcendentals=0),
-    )(info, *operands)
-
-
-def start(info, x, gain, shift, w_qkv, query_bias, value_bias):
+    )(*scalars, *operands)
+
+
+def start(x, gain, shift, w_qkv, query_bias, value_bias):
     rows, width = x.shape
-    shapes = [jax.ShapeDtypeStruct((GROUPS, rows + rows // LANES * HEAD_DIM, LANES), BF16)] * GROUP_HEADS
+    height = rows + rows // LANES * HEAD_DIM
+    shapes = [jax.ShapeDtypeStruct((GROUPS, n * height, LANES), BF16) for n in (1, GROUP_HEADS - 1)]
     operands = (x, gain, shift, w_qkv, query_bias, value_bias)
-    return one_step(start_kernel, info, operands, shapes, [], 2 * rows * width * 3 * width)
+    return one_step(start_kernel, None, operands, shapes, [], 2 * rows * width * 3 * width)
 
 
 def middle_kernel(
-    info_ref, x_ref, out_grad_ref, keep_ref, w_proj_ref, proj_bias_ref, gain_ref, shift_ref, w_fc1_ref, fc1_bias_ref, w_fc2_ref,
+    x_ref, out_grad_ref, keep_ref, w_proj_ref, proj_bias_ref, gain_ref, shift_ref, w_fc1_ref, fc1_bias_ref, w_fc2_ref,
     fc2_bias_ref, *refs,
 ):
     attended_refs, refs = refs[:GROUP_HEADS], refs[GROUP_HEADS:]
@@ -588,7 +573,7 @@
     grad_ref[...] = back_attended.reshape(grad_ref.shape)
 
 
-def middle(info, x, out_grad, keep, w_proj, proj_bias, gain, shift, w_fc1, fc1_bias, w_fc2, fc2_bias, attended):
+def middle(x, out_grad, keep, w_proj, proj_bias, gain, shift, w_fc1, fc1_bias, w_fc2, fc2_bias, attended):
     rows, width = x.shape
     ff = w_fc1.shape[1]
     low = lambda *shape: jax.ShapeDtypeStruct(shape, BF16)
@@ -600,7 +585,7 @@
     operands = [x, out_grad, keep, w_proj, proj_bias, gain, shift, w_fc1, fc1_bias, w_fc2, fc2_bias]
     operands += attended
     scratch = [pltpu.VMEM((HEADS, HEAD_DIM, rows), BF16)]
-    outs = one_step(middle_kernel, info, operands, shapes, scratch, 2 * rows * width * (2 * width + 4 * ff))
+    outs = one_step(middle_kernel, None, operands, shapes, scratch, 2 * rows * width * (2 * width + 4 * ff))
     return outs[0], outs[1], outs[2:9], outs[9]
 
 
@@ -641,7 +626,7 @@
     put(at, dot32(jnp.ones((8, rows), BF16), query, (1, 1))[0:1])
     put(at + per, jnp.sum(flat[:, width:].astype(F32), axis=0, keepdims=True))
     lines[at + 2 * per :, :] = jnp.zeros((lines.shape[0] - at - 2 * per, LANES), F32)
-    core = info_ref[1] % 2
+    core = info_ref[0] % 2
 
     def window(step, _):
         for ref, which in ((send_ref, 1 - core), (keep_ref, core)):
@@ -673,36 +658,38 @@
     return lax.optimization_barrier((values, list(after)))[0] if len(after) > 0 else values
 
 
+def exchange(parts):
+    return [lax.ppermute(part, ("x", "c"), [(i, i ^ n) for i in range(4)]) for part, n in zip(parts, (2, 1, 3))]
+
+
 class Plane:
-    parts = (2, 2)
-
     def gather_keys(self, kv):
         return [kv[None], swap(kv, "f")[None]]
 
     def gather_queries(self, q):
-        over = swap(q, "x")
-        return [q, over, swap(q, "c"), swap(over, "c")]
+        return [q] + exchange([q] * 3)
 
     gather_grads = gather_queries
 
-    def merge(self, outs):
-        mine, sent = merge_cores(outs[0], swap(outs[1], "c"))
-        yield [sent]
-        yield merge_chips(mine, swap(sent, "x"))
-
-    def sum_back(self, outs):
-        q_sent, q_kept, sent, kept = outs[1], outs[0], outs[3][0], outs[2][0]
-        both = add(q_kept, swap(q_sent, "c"))
-        groups, clips, rows, _ = kept.shape
-        came = swap(sent, "f").reshape(groups, clips * rows, PAIR)
-        return sum_back(kept.reshape(groups, clips * rows, PAIR), came, both[0], swap(both[1], "x"))
+    def gather_first(self, values):
+        over = swap(values, "x")
+        return [values, over, swap(values, "c"), swap(over, "c")]
+
+    def gather_parts(self, outs):
+        return [outs[0]] + exchange(outs[1:4])
+
+    def gather_back(self, outs):
+        kept, sent = outs[4][0], outs[5][0]
+        shape = (kept.shape[0], -1, PAIR)
+        return kept.reshape(shape), swap(sent, "f").reshape(shape), self.gather_parts(outs)
+
+    def sum_back(self, after, parts):
+        return sum_back(after, *parts)
 
 
 class AnyPlane:
-    parts = (1,)
-
-    def __init__(self, clips, times):
-        self.clips, self.times = clips, times
+    def __init__(self, clips, times, part):
+        self.clips, self.times, self.part = clips, times, part
 
     def split(self, values):
         groups, rows, width = values.shape
@@ -714,27 +701,24 @@
 
     def gather_queries(self, q):
         groups, tiles, rows, lanes = q.shape
-        q = lax.all_gather(q.transpose(0, 2, 1, 3).reshape(groups, rows, self.clips, -1), "t")
-        return [q.transpose(1, 3, 2, 0, 4).reshape(groups, self.clips, rows, -1)]
+        q = lax.all_gather(q.transpose(0, 2, 1, 3).reshape(groups, rows, -1, self.part), "t")
+        return [q.transpose(1, 3, 2, 0, 4).reshape(groups, -1, rows, self.times * self.part)]
 
     def gather_grads(self, values):
         groups, rows, _ = values.shape
-        values = lax.all_gather(values.reshape(groups, rows, self.clips, -1), "t")
+        values = lax.all_gather(values.reshape(groups, rows, -1, self.part), "t")
         return [values.transpose(1, 2, 3, 0, 4).reshape(groups, rows, -1)]
 
-    def merge(self, outs):
-        came = lax.all_to_all(self.split(outs[0][0]), "t", 0, 0, tiled=True)
-        out, lse = came[:, :, :HEAD_DIM], came[:, :, HEAD_DIM : HEAD_DIM + 1]
-        most = jnp.max(lse, axis=0)
-        share = jnp.exp2(lse - most)
-        total = jnp.sum(share, axis=0)
-        out = jnp.sum(out * share, axis=0) / total
-        lse = jnp.broadcast_to(most + jnp.log2(total), (GROUPS, OUT_ROWS - HEAD_DIM, out.shape[-1]))
-        yield [out]
-        yield jnp.concatenate([out, lse], axis=1), out.astype(BF16)
-
-    def sum_back(self, outs):
-        back_q = lax.psum_scatter(self.split(outs[0][0]), "t", scatter_dimension=0, tiled=False)
+    gather_first = gather_grads
+
+    def gather_parts(self, outs):
+        return list(lax.all_to_all(self.split(outs[0]), "t", 0, 0, tiled=True))
+
+    def gather_back(self, outs):
+        return outs
+
+    def sum_back(self, after, outs):
+        back_q = lax.psum_scatter(self.split(outs[0]), "t", scatter_dimension=0, tiled=False)
         back_kv = lax.psum_scatter(outs[1], "f", scatter_dimension=0, tiled=False).reshape(GROUPS, -1, PAIR)
         back_q = back_q.reshape(GROUPS, HEAD_DIM, -1, LANES).transpose(0, 2, 1, 3).reshape(GROUPS, -1, LANES)
         return jnp.concatenate([back_kv, back_q], axis=1)
@@ -779,57 +763,51 @@
     devices = lax.axis_size("f") * GROUPS * times
     early_index = lax.axis_index(time_axes)
     fast = time_axes == ("x", "c")
-    plane = Plane() if fast else AnyPlane(clips, times)
-    core = lax.axis_index(time_axes[-1]).reshape(1)
+    plane = Plane() if fast else AnyPlane(clips, times, part)
     first_frame = (lax.axis_index("g") * times + early_index) * frames
     frame = first_frame + lax.broadcasted_iota(jnp.int32, (1, freq_rows, frames), 2)
     keep_rows = (frame < lengths[:, None, None]).astype(F32).reshape(rows, 1)
-    info = [lax.axis_index("g"), early_index]
-    for clip in range(clips):
-        info += [lengths[clip] // frames, lengths[clip] % frames]
-    info = jnp.stack(info).astype(jnp.int32)
+    info = jnp.concatenate([early_index.astype(jnp.int32).reshape(1), lengths])
 
     x = tokens.reshape(rows, width)
-    packs = start(info, x, norm1_gain, norm1_shift, w_qkv, query_bias, value_bias)
-    kv, q, attended, kept, merges, outs = [], [], [], [], [], ()
-
-    def fetch(head, after):
-        got = along_g(packs[head])
-        pairs, queries = hold((got[:, :rows], got[:, rows:]), after)
-        kv.append(plane.gather_keys(pairs.reshape(GROUPS, clips, part, PAIR)))
-        q.append(plane.gather_queries(queries.reshape(GROUPS, -1, HEAD_DIM, LANES)))
-
-    def merged(merge):
-        out, low = next(merge)
+    packs = start(x, norm1_gain, norm1_shift, w_qkv, query_bias, value_bias)
+    attended, kept = [], []
+
+    def fetch(values, heads, after):
+        got = along_g(values)
+        pairs, queries = hold((got[:, : heads * rows], got[:, heads * rows :]), after)
+        kv = plane.gather_keys(pairs.reshape(GROUPS, heads * clips, part, PAIR))
+        return kv, plane.gather_queries(queries.reshape(GROUPS, -1, HEAD_DIM, LANES))
+
+    def merged(after, parts):
+        out, low = merge(parts, after)
         kept.append(out)
         attended.append(along_g(low))
         return low
 
+    def run(head, clip, outs, after):
+        kv, q = fetched[min(head, 1)]
+        place = max(head - 1, 0) * clips + clip
+        *outs, token = attend(info, kv, q, place, clip, clips, times, frames, outs, after)
+        return outs, token
+
+    fetched = [fetch(packs[0], 1, [])]
+    fetched.append(fetch(packs[1], GROUP_HEADS - 1, fetched[0][0][1:] + fetched[0][1][1:]))
+    parts = None
     for head in range(GROUP_HEADS):
-        for later in {0: (0, 1), 1: (2,)}.get(head, ()):
-            fetch(later, [outs[0]] if later > 1 else [])
-        for clip in range(clips):
-            after = []
-            if clip == 0 and head > 0:
-                merges.append(plane.merge(outs))
-                after = [outs[0]]
-                outs = ()
-                if head > 1:
-                    after.append(merged(merges[-2]))
-            if clip == clips - 1:
-                if head > 0:
-                    after = next(merges[-1])
-                if fast and head + 1 < GROUP_HEADS:
-                    after += [q[head + 1][1]]
-            outs = attend(info, kv[head], q[head], clip, clips, times, frames, plane.parts, outs, after)
-    merges.append(plane.merge(outs))
-    next(merges[-1])
-    for merge in merges[len(attended) :]:
-        merged(merge)
+        outs, token = run(head, 0, (), [] if head == 0 else [token])
+        after = [token]
+        if head > 0:
+            after.append(merged(token, parts))
+        for clip in range(1, clips):
+            outs, token = run(head, clip, outs, after)
+        come = fetched[1][0][1:] + fetched[1][1][1:] if head == 0 else []
+        parts = plane.gather_parts(hold(outs, come))
+    merged(token, parts)
     if fast:
         size = moment.shape[0] // LANES
         block_out, back_hidden, early, grad = middle(
-            info, x, out_grad.reshape(rows, width), keep_rows, w_proj, proj_bias, norm2_gain, norm2_shift, w_fc1, fc1_bias,
+            x, out_grad.reshape(rows, width), keep_rows, w_proj, proj_bias, norm2_gain, norm2_shift, w_fc1, fc1_bias,
             w_fc2, fc2_bias, attended,
         )
         block_out = block_out.reshape(tokens.shape)
@@ -860,30 +838,46 @@
         early_windows = info
         grad = back_attended.reshape(GROUPS, -1, rows)
     ready = grad_rows_of(along_g(grad), kept, early_windows)
-    back, outs = [], ()
+    back, parts, token = [], None, None
+    grads = plane.gather_first(ready[0])
+    if fast:
+        early_sum = hold(early_windows, grads[:1]).reshape(2, 2, 2, GROUPS, EARLY_WINDOW, LANES)
+        early_sum = lax.psum_scatter(early_sum, "c", scatter_dimension=0, tiled=False)
+
+    def run_back(head, clip, outs, after):
+        kv, q = fetched[min(head, 1)]
+        place = max(head - 1, 0) * clips + clip
+        *outs, token = attend_back(info, kv, q, grads, place, clip, clips, times, frames, outs, after)
+        return outs, token
+
     for head in range(GROUP_HEADS):
-        grads = plane.gather_grads(hold(ready[head], one) if head > 0 else ready[head])
+        outs, token = run_back(head, 0, (), [] if head == 0 else [token])
+        after = [token]
+        if head > 0:
+            after.append(plane.sum_back(token, parts))
+            back.append(along_g(after[-1]))
         if fast and head == 0:
-            early_sum = hold(early_windows, grads)
-            early_sum = lax.psum_scatter(early_sum, ("f", "g") + time_axes, scatter_dimension=0, tiled=False)
-        before, outs = outs, ()
-        for clip in range(clips):
-            after = []
-            if head > 0 and clip == 0:
-                after = [before[0]]
-            elif head > 0:
-                after = [plane.sum_back(before)]
-                back.append(along_g(after[0]))
-            outs = attend_back(info, kv[head], q[head], grads, clip, clips, times, frames, plane.parts, outs, after)
-            one = [outs[0]] if clip == 0 else one
-    back.append(along_g(plane.sum_back(outs)))
+            early_sum = hold(early_sum, [token])
+            after.append(early_sum)
+            early_sum = early_sum.reshape(4, GROUPS, EARLY_WINDOW, LANES)
+            early_sum = lax.psum_scatter(early_sum, ("x", "f"), scatter_dimension=0, tiled=False)
+        if head + 1 < GROUP_HEADS:
+            later = plane.gather_grads(hold(ready[head + 1], after))
+        for clip in range(1, clips):
+            outs, token = run_back(head, clip, outs, after)
+        if head + 1 < GROUP_HEADS:
+            outs = hold(outs, later[1:])
+            grads = later
+        parts = plane.gather_back(outs)
+    back.append(along_g(plane.sum_back(token, parts)))
     if fast:
         input_grad, *late_windows = finish(
             size, info, x, norm1_gain, norm1_shift, w_qkv, back_hidden, back
         )
         input_grad = input_grad.reshape(tokens.shape)
-        late_sum = reduce_late(*late_windows)
-        weight_grad = own_chunk(lax.optimization_barrier(early_sum.astype(F32)), late_sum, moment.shape[0])
+        early_sum = lax.psum_scatter(hold(early_sum, [back[-1]]), "g", scatter_dimension=0, tiled=False).astype(F32)
+        late_sum = reduce_late(*late_windows, early_sum)
+        weight_grad = own_chunk(lax.optimization_barrier(early_sum), late_sum, moment.shape[0])
     else:
         back = jnp.stack(back, axis=1)
         back_kv = back[:, :, :rows].transpose(2, 0, 1, 3).reshape(rows, 2 * width)

time: 649 us -> 601 us (0.926)
  starting transfers between devices: 88.9 us -> 67.4 us
  waiting for transfers between devices: 137 us -> 118 us
  blocking collectives: 50.7 us -> 68.4 us
  local copies, waits for them, and re-layouts: 24 us -> 11.6 us
  Pallas kernels: 330 us -> 322 us
    ppermute x42 -> x14, waiting for transfers between devices: 114 us -> 31.8 us  [swap(): return lax.ppermute(values, axis, SWAP)]
    ppermute x3 -> x31, waiting for transfers between devices: 3.33 us -> 35.8 us  [the longest x30 28.6 us: exchange(): lax.ppermute(part, ('x', 'c'), [(i, i ^ n) for i in range(4)])]
    all_to_all x8 -> x7, waiting for transfers between devices: 19.6 us -> 39.8 us  [along_g(): return lax.all_to_all(values, 'g', 0, 0, tiled=True)]
    all_to_all x2 -> x3, blocking collectives: 50.7 us -> 68.4 us  [along_g(): return lax.all_to_all(values, 'g', 0, 0, tiled=True)]
    ppermute x42 -> x14, starting transfers between devices: 26.6 us -> 13.9 us  [swap(): return lax.ppermute(values, axis, SWAP)]
    reduce_scatter x1 -> x2, waiting for transfers between devices: 0.02 us -> 10.2 us  [the longest x1 10.2 us: per_device(): lax.psum_scatter(hold(early_sum, [back[-1]]), 'g', scatter_dimension=0, t...]
    all_to_all x8 -> x7, starting transfers between devices: 38.1 us -> 29.8 us  [along_g(): return lax.all_to_all(values, 'g', 0, 0, tiled=True)]
    unnamed x100 -> x94, local copies, waits for them, and re-layouts: 16.7 us -> 9.39 us
  transfers between devices with their start and end apart: 54 -> 55, of which waited for: 22 -> 18; matrix products, arithmetic and copies ran while one was open for 1% -> 1% of each run, Pallas kernels for 41% -> 47%
where the time goes in v1:
time: 601 us; the launch traced here: 608 us
  Pallas kernels  322 us (54%)
  waiting for transfers between devices  118 us (20%)
  blocking collectives  68.4 us (11%)
  starting transfers between devices  67.4 us (11%)
  between operations  15.4 us (3%)
  local copies, waits for them, and re-layouts  11.6 us (2%)
    pallas_call x6, Pallas kernels, attend_back(): pl.pallas_call(functools.partial(attend_back_kernel, clip, times, frames,...  160 us
    pallas_call x6, Pallas kernels, attend(): pl.pallas_call(functools.partial(attend_kernel, clip, times, frames, len(...  75 us
    all_to_all x3, blocking collectives, along_g(): return lax.all_to_all(values, 'g', 0, 0, tiled=True)  68.4 us
    pallas_call x3, Pallas kernels, one_step(): pl.pallas_call(kernel, grid_spec=pltpu.PrefetchScalarGridSpec(num_scalar_...  42 us
    all_to_all x7, waiting for transfers between devices, along_g(): return lax.all_to_all(values, 'g', 0, 0, tiled=True)  39.8 us
    ppermute x14, waiting for transfers between devices, swap(): return lax.ppermute(values, axis, SWAP)  31.8 us
    all_to_all x7, starting transfers between devices, along_g(): return lax.all_to_all(values, 'g', 0, 0, tiled=True)  29.8 us
    ppermute x30, waiting for transfers between devices, exchange(): lax.ppermute(part, ('x', 'c'), [(i, i ^ n) for i in range(4)])  28.6 us
  transfers between devices with their start and end apart: 55, of which 18 were waited for; matrix products, arithmetic and copies ran while one was open for 1% of the time, Pallas kernels for 47%

profile of v1, /device:TPU:0, one launch (start us, length us, event | category | flops | bytes accessed | tf_op | source)
XLA Modules:
  0.0 608.0 jit_solution(645697692171369594)
XLA Ops:
  7.2 6.1 %shard_map.201 = (bf16[4,768,128]{2,1,0:T(8,128)(2,1)}, bf16[4,1536,128]{2,1,0:T(8,128)(2,1)}) custom-call(bf16[512,768]{1,0:T(8,128)(2,1)} %bitcast.114, f32[768]{0:T(1024)} %gain_ref.5, f32[768]{0:T(1024)} %shift_ref.5, bf16[768,2304]{1,0:T(8,128)(2,1)} %w_ref.3, f32[768]{0:T(1024)} %query_bias_ref.1, f32[768]{0:T(1024)} %value_bias_ref.1), custom_call_target="tpu_custom_call" | custom-call | flops 1811939328 | bytes 3623878 | tf_op jit(solution)/shard_map/pallas_call | solution.py:498
  13.3 26.4 %all_to_all.50 = bf16[4,768,128]{2,1,0:T(8,128)(2,1)S(1)} all-to-all(bf16[4,768,128]{2,1,0:T(8,128)(2,1)} %get-tuple-element.125), channel_id=1, replica_groups=mesh['f'=2,'g'=4,'x'=2,'c'=2] {'g'}, dimensions={0} | all-to-all | bytes 1572864 | tf_op jit(solution)/shard_map/all_to_all | solution.py:654
  39.7 3.6 all-to-all-start
  47.9 31.5 %all-to-all-done = bf16[4,1536,128]{2,1,0:T(8,128)(2,1)S(1)} async-done(((bf16[4,1536,128]{2,1,0:T(8,128)(2,1)}), bf16[4,1536,128]{2,1,0:T(8,128)(2,1)S(1)}, u32[]{:S(2)}, u32[]{:S(2)}) %all-to-all-start) | async-done | bytes 1572896 | tf_op jit(solution)/shard_map/all_to_all | solution.py:654
  83.9 12.5 %shard_map.202 = (bf16[4,80,512]{2,1,0:T(8,128)(2,1)}, bf16[4,80,512]{2,1,0:T(8,128)(2,1)}, bf16[4,80,512]{2,1,0:T(8,128)(2,1)}, bf16[4,80,512]{2,1,0:T(8,128)(2,1)}, f32[8,128]{1,0:T(8,128)}) custom-call(s32[3]{0:T(128)} %pad_add_fusion.info_ref, bf16[1,4,2,256,128]{4,3,2,1,0:T(8,128)(2,1)} %bitcast.10.refs_0_, ...), custom_call_target="tpu_custom_call" | custom-call | flops 2147483648 | bytes 524288 | tf_op jit(solution)/shard_map/pallas_call | solution.py:142
  96.3 12.5 %shard_map.203 = (bf16[4,80,512]{2,1,0:T(8,128)(2,1)}, bf16[4,80,512]{2,1,0:T(8,128)(2,1)}, bf16[4,80,512]{2,1,0:T(8,128)(2,1)}, bf16[4,80,512]{2,1,0:T(8,128)(2,1)}, f32[8,128]{1,0:T(8,128)}) custom-call(s32[3]{0:T(128)} %pad_add_fusion.info_ref, ...), custom_call_target="tpu_custom_call", output_to_operand_aliasing={{0}: (7, {}), {1}: (8, {}), {2}: (9, {}), {3}: (10, {})} | custom-call | flops 2147483648 | bytes 524288 | tf_op jit(solution)/shard_map/pallas_call | solution.py:142
  111.7 12.7 %shard_map.204 = (bf16[4,80,512]{2,1,0:T(8,128)(2,1)}, bf16[4,80,512]{2,1,0:T(8,128)(2,1)}, bf16[4,80,512]{2,1,0:T(8,128)(2,1)}, bf16[4,80,512]{2,1,0:T(8,128)(2,1)}, f32[8,128]{1,0:T(8,128)}) custom-call(s32[3]{0:T(128)} %pad_add_fusion.info_ref, bf16[1,4,4,256,128]{4,3,2,1,0:T(8,128)(2,1)} %bitcast.71, bf16[1,4,4,256,128]{4,3,2,1,0:T(8,128)(2,1)} %bitcast.105, ...), custom_call_target="tpu_custom_call" | custom-call | flops 2147483648 | bytes 524288 | tf_op jit(solution)/shard_map/pallas_call | solution.py:142
  124.5 2.3 collective-permute-done.10.refs_3_
  127.5 2.5 shard_map.205
  129.9 3.4 all-to-all-start.2
  133.4 12.5 %shard_map.206 = (bf16[4,80,512]{2,1,0:T(8,128)(2,1)}, bf16[4,80,512]{2,1,0:T(8,128)(2,1)}, bf16[4,80,512]{2,1,0:T(8,128)(2,1)}, bf16[4,80,512]{2,1,0:T(8,128)(2,1)}, f32[8,128]{1,0:T(8,128)}) custom-call(s32[3]{0:T(128)} %pad_add_fusion.info_ref, ...), custom_call_target="tpu_custom_call", output_to_operand_aliasing={{0}: (7, {}), {1}: (8, {}), {2}: (9, {}), {3}: (10, {})} | custom-call | flops 2147483648 | bytes 524288 | tf_op jit(solution)/shard_map/pallas_call | solution.py:142
  148.0 12.5 %shard_map.207 = (bf16[4,80,512]{2,1,0:T(8,128)(2,1)}, bf16[4,80,512]{2,1,0:T(8,128)(2,1)}, bf16[4,80,512]{2,1,0:T(8,128)(2,1)}, bf16[4,80,512]{2,1,0:T(8,128)(2,1)}, f32[8,128]{1,0:T(8,128)}) custom-call(s32[3]{0:T(128)} %pad_add_fusion.info_ref, bf16[1,4,4,256,128]{4,3,2,1,0:T(8,128)(2,1)} %bitcast.73, bf16[1,4,4,256,128]{4,3,2,1,0:T(8,128)(2,1)} %bitcast.107, ...), custom_call_target="tpu_custom_call" | custom-call | flops 2147483648 | bytes 524288 | tf_op jit(solution)/shard_map/pallas_call | solution.py:142
  162.7 2.5 shard_map.208
  165.2 4.8 all-to-all-start.3
  170.0 12.5 %shard_map.209 = (bf16[4,80,512]{2,1,0:T(8,128)(2,1)}, bf16[4,80,512]{2,1,0:T(8,128)(2,1)}, bf16[4,80,512]{2,1,0:T(8,128)(2,1)}, bf16[4,80,512]{2,1,0:T(8,128)(2,1)}, f32[8,128]{1,0:T(8,128)}) custom-call(s32[3]{0:T(128)} %pad_add_fusion.info_ref, ...), custom_call_target="tpu_custom_call", output_to_operand_aliasing={{0}: (7, {}), {1}: (8, {}), {2}: (9, {}), {3}: (10, {})} | custom-call | flops 2147483648 | bytes 524288 | tf_op jit(solution)/shard_map/pallas_call | solution.py:142
  184.6 8.6 %collective-permute-done.14.refs_1_ = bf16[4,80,512]{2,1,0:T(8,128)(2,1)S(1)} collective-permute-done((bf16[4,80,512]{2,1,0:T(8,128)(2,1)}, bf16[4,80,512]{2,1,0:T(8,128)(2,1)S(1)}, u32[]{:S(2)}, u32[]{:S(2)}) %collective-permute-start.14) | collective-permute-done | bytes 327712 | tf_op jit(solution)/shard_map/ppermute | solution.py:662
  193.2 5.6 collective-permute-done.16.refs_3_
  199.6 2.5 shard_map.210
  202.1 5.0 all-to-all-start.4
  208.1 8.3 %all-to-all-done.4.refs_2_ = bf16[4,64,512]{2,1,0:T(8,128)(2,1)S(1)} async-done(((bf16[4,64,512]{2,1,0:T(8,128)(2,1)}), bf16[4,64,512]{2,1,0:T(8,128)(2,1)S(1)}, u32[]{:S(2)}, u32[]{:S(2)}) %all-to-all-start.4) | async-done | bytes 262176 | tf_op jit(solution)/shard_map/all_to_all | solution.py:654
  217.1 22.6 %shard_map.211 = (bf16[512,768]{1,0:T(8,128)(2,1)}, f32[512,768]{1,0:T(8,128)}, bf16[768,512]{1,0:T(8,128)(2,1)}, bf16[512,768]{1,0:T(8,128)(2,1)}, bf16[512,768...) custom-call(bf16[512,768]{1,0:T(8,128)(2,1)} %bitcast.115, ...), custom_call_target="tpu_custom_call" | custom-call | flops 10871635968 | bytes 21743272 | tf_op jit(solution)/shard_map/pallas_call | solution.py:498
  239.7 3.5 all-to-all-start.5
  243.2 26.5 %shard_map.212.refs_3_ = bf16[32,1744,128]{2,1,0:T(8,128)(2,1)} custom-call(bf16[768,512]{1,0:T(8,128)(2,1)} %get-tuple-element.171.att_ref, bf16[512,768]{1,0:T(8,128)(2,1)} %get-tuple-element.172.branch_ref, bf16[512,768]{1,0:T(8,128)(2,1)} %get-tuple-element.173.normed_ref, bf16[512,3072]{1,0:T(8,128)(2,1)} %get-tuple-element.174.pre_ref, ...), custom_call_target="tpu_custom_call" | custom-call | flops 5445255168 | bytes 21270528 | tf_op jit(solution)/shard_map/pallas_call | solution.py:396
  270.6 2.7 shard_map.213
  276.0 6.0 collective-permute-done.17.refs_7_
  284.9 27.0 %shard_map.214 = (bf16[4,64,512]{2,1,0:T(8,128)(2,1)}, bf16[4,64,512]{2,1,0:T(8,128)(2,1)}, bf16[4,64,512]{2,1,0:T(8,128)(2,1)}, bf16[4,64,512]{2,1,0:T(8,128)(2...) custom-call(s32[3]{0:T(128)} %pad_add_fusion.info_ref, ...), custom_call_target="tpu_custom_call" | custom-call | flops 5368709120 | bytes 1048576 | tf_op jit(solution)/shard_map/pallas_call | solution.py:235
  315.0 26.5 %shard_map.215 = (bf16[4,64,512]{2,1,0:T(8,128)(2,1)}, bf16[4,64,512]{2,1,0:T(8,128)(2,1)}, bf16[4,64,512]{2,1,0:T(8,128)(2,1)}, bf16[4,64,512]{2,1,0:T(8,128)(2...) custom-call(s32[3]{0:T(128)} %pad_add_fusion.info_ref, ...), custom_call_target="tpu_custom_call", output_to_operand_aliasing={{0}: (11, {}), {1}: (12, {}), {2}: (13, {}), {3}: (14, {}),... | custom-call | flops 5368709120 | bytes 1048576 | tf_op jit(solution)/shard_map/pallas_call | solution.py:235
  344.2 26.8 %shard_map.216 = (bf16[4,64,512]{2,1,0:T(8,128)(2,1)}, bf16[4,64,512]{2,1,0:T(8,128)(2,1)}, bf16[4,64,512]{2,1,0:T(8,128)(2,1)}, bf16[4,64,512]{2,1,0:T(8,128)(2...) custom-call(s32[3]{0:T(128)} %pad_add_fusion.info_ref, ...), custom_call_target="tpu_custom_call" | custom-call | flops 5368709120 | bytes 1048576 | tf_op jit(solution)/shard_map/pallas_call | solution.py:235
  372.1 2.7 shard_map.217.refs_17_
  374.7 4.5 all-to-all-start.6
  381.4 26.5 %shard_map.218 = (bf16[4,64,512]{2,1,0:T(8,128)(2,1)}, bf16[4,64,512]{2,1,0:T(8,128)(2,1)}, bf16[4,64,512]{2,1,0:T(8,128)(2,1)}, bf16[4,64,512]{2,1,0:T(8,128)(2...) custom-call(s32[3]{0:T(128)} %pad_add_fusion.info_ref, ...), custom_call_target="tpu_custom_call", output_to_operand_aliasing={{0}: (11, {}), {1}: (12, {}), {2}: (13, {}), {3}: (14, {}),... | custom-call | flops 5368709120 | bytes 1048576 | tf_op jit(solution)/shard_map/pallas_call | solution.py:235
  411.2 26.7 %shard_map.219 = (bf16[4,64,512]{2,1,0:T(8,128)(2,1)}, bf16[4,64,512]{2,1,0:T(8,128)(2,1)}, bf16[4,64,512]{2,1,0:T(8,128)(2,1)}, bf16[4,64,512]{2,1,0:T(8,128)(2...) custom-call(s32[3]{0:T(128)} %pad_add_fusion.info_ref, ...), custom_call_target="tpu_custom_call" | custom-call | flops 5368709120 | bytes 1048576 | tf_op jit(solution)/shard_map/pallas_call | solution.py:235
  439.0 2.6 shard_map.220.refs_17_
  441.6 5.1 all-to-all-start.7
  446.7 26.5 %shard_map.221 = (bf16[4,64,512]{2,1,0:T(8,128)(2,1)}, bf16[4,64,512]{2,1,0:T(8,128)(2,1)}, bf16[4,64,512]{2,1,0:T(8,128)(2,1)}, bf16[4,64,512]{2,1,0:T(8,128)(2...) custom-call(s32[3]{0:T(128)} %pad_add_fusion.info_ref, ...), custom_call_target="tpu_custom_call", output_to_operand_aliasing={{0}: (11, {}), {1}: (12, {}), {2}: (13, {}), {3}: (14, {}),... | custom-call | flops 5368709120 | bytes 1048576 | tf_op jit(solution)/shard_map/pallas_call | solution.py:235
  476.3 7.3 %collective-permute-done.35.refs_1_ = bf16[4,64,512]{2,1,0:T(8,128)(2,1)S(1)} collective-permute-done((bf16[4,64,512]{2,1,0:T(8,128)(2,1)}, bf16[4,64,512]{2,1,0:T(8,128)(2,1)S(1)}, u32[]{:S(2)}, u32[]{:S(2)}) %collective-permute-start.35) | collective-permute-done | bytes 262176 | tf_op jit(solution)/shard_map/ppermute | solution.py:662
  483.6 3.2 collective-permute-done.37.refs_3_
  487.9 2.6 shard_map.222
  490.5 26.0 %all_to_all.51.refs_2_ = bf16[4,768,128]{2,1,0:T(8,128)(2,1)} all-to-all(bf16[4,768,128]{2,1,0:T(8,128)(2,1)} %shard_map.222), channel_id=1, replica_groups=mesh['f'=2,'g'=4,'x'=2,'c'=2] {'g'}, dimensions={0} | all-to-all | bytes 1572864 | tf_op jit(solution)/shard_map/all_to_all | solution.py:654
  516.5 13.4 %shard_map.223 = (bf16[512,768]{1,0:T(8,128)(2,1)}, bf16[4,1792,128]{2,1,0:T(8,128)(2,1)}, bf16[4,1792,128]{2,1,0:T(8,128)(2,1)}) custom-call(s32[3]{0:T(128)} %pad_add_fusion.info_ref, bf16[512,768]{1,0:T(8,128)(2,1)} %bitcast.116, f32[768]{0:T(1024)} %gain_ref.5, f32[768]{0:T(1024)} %shift_ref.5, bf16[768,2304]{1,0:T(8,128)(2,1)} %w_ref.3, ...), custom_call_target="tpu_custom_call" | custom-call | flops 3623878656 | bytes 7247757 | tf_op jit(solution)/shard_map/pallas_call | solution.py:498
  529.9 4.0 collective-permute-done.38
  533.9 2.3 add_convert_fusion
  539.0 9.9 %collective-permute-done.41 = bf16[2,2,448,128]{3,2,0,1:T(8,128)(2,1)S(1)} collective-permute-done((bf16[2,2,448,128]{3,2,0,1:T(8,128)(2,1)S(1)}, bf16[2,2,448,128]{3,2,0,1:T(8,128)(2,1)S(1)}, u32[]{:S(2)}, u32[]{:S(2)}) %collective-permute-start.41) | collective-permute-done | bytes 458784 | tf_op jit(solution)/shard_map/ppermute | solution.py:412
  551.8 4.1 collective-permute-done.42
  557.6 10.2 %reduce-scatter.8.cloned.1.call-done = bf16[1,1744,128]{2,1,0:T(8,128)(2,1)} async-done(((bf16[4,1744,128]{2,1,0:T(8,128)(2,1)}), bf16[1,1744,128]{2,1,0:T(8,128)(2,1)}) %reduce-scatter.8.cloned.1.call-update) | async-done | bytes 446480 | tf_op jit(solution)/shard_map/reduce_scatter | solution.py:878
  568.9 16.0 %all_to_all.52 = bf16[4,448,128]{2,1,0:T(8,128)(2,1)S(1)} all-to-all(bf16[4,448,128]{2,1,0:T(8,128)(2,1)S(1)} %pad_maximum_fusion), channel_id=1, replica_groups=mesh['f'=2,'g'=4,'x'=2,'c'=2] {'g'}, dimensions={0} | all-to-all | bytes 917504 | tf_op jit(solution)/shard_map/all_to_all | solution.py:654
  586.2 7.3 %collective-permute-done.43 = bf16[448,128]{1,0:T(8,128)(2,1)S(1)} collective-permute-done((bf16[448,128]{1,0:T(8,128)(2,1)S(1)}, bf16[448,128]{1,0:T(8,128)(2,1)S(1)}, u32[]{:S(2)}, u32[]{:S(2)}) %collective-permute-start.43) | collective-permute-done | bytes 114720 | tf_op jit(solution)/shard_map/ppermute | solution.py:437
  595.5 4.2 collective-permute-done.44
  (210 shorter events, 58.0 us)
Async XLA Ops:
  39.7 39.6 %all-to-all-start = ((bf16[4,1536,128]{2,1,0:T(8,128)(2,1)}), bf16[4,1536,128]{2,1,0:T(8,128)(2,1)S(1)}, u32[]{:S(2)}, u32[]{:S(2)}) async-start(bf16[4,1536,128]{2,1,0:T(8,128)(2,1)} %get-tuple-element.124), calls=%async_computation | async-start | bytes 3145728 | tf_op jit(solution)/shard_map/all_to_all | solution.py:654
  44.1 35.4 %collective-permute-start = (bf16[4,2,256,128]{3,2,1,0:T(8,128)(2,1)}, bf16[4,2,256,128]{3,2,1,0:T(8,128)(2,1)}, u32[]{:S(2)}, u32[]{:S(2)}) collective-permute-start(bf16[4,2,256,128]{3,2,1,0:T(8,128)(2,1)} %bitcast.3), channel_id=1, source_target_pairs={{0,16},{16,0},{1,17},{17,1},{2,18},{18,2},{3,19},{19,3},{4,20},{20... | collective-permute-start | bytes 1572872 | tf_op jit(solution)/shard_map/ppermute | solution.py:412
  45.7 33.8 %collective-permute-start.1 = (bf16[4,4,64,128]{3,2,1,0:T(8,128)(2,1)S(1)}, bf16[4,4,64,128]{3,2,1,0:T(8,128)(2,1)}, u32[]{:S(2)}, u32[]{:S(2)}) collective-permute-start(bf16[4,4,64,128]{3,2,1,0:T(8,128)(2,1)S(1)} %bitcast.98), channel_id=1, source_target_pairs={{0,2},{1,3},{2,0},{3,1},{4,6},{5,7},{6,4},{7,5},{8,10},{9,11},{10,... | collective-permute-start | bytes 786440 | tf_op jit(solution)/shard_map/ppermute | solution.py:662
  47.2 32.3 %collective-permute-start.2 = (bf16[4,4,64,128]{3,2,1,0:T(8,128)(2,1)S(1)}, bf16[4,4,64,128]{3,2,1,0:T(8,128)(2,1)}, u32[]{:S(2)}, u32[]{:S(2)}) collective-permute-start(bf16[4,4,64,128]{3,2,1,0:T(8,128)(2,1)S(1)} %bitcast.99), channel_id=1, source_target_pairs={{0,1},{1,0},{2,3},{3,2},{4,5},{5,4},{6,7},{7,6},{8,9},{9,8},{10,11... | collective-permute-start | bytes 786440 | tf_op jit(solution)/shard_map/ppermute | solution.py:662
  47.2 32.3 %collective-permute-start.3 = (bf16[4,4,64,128]{3,2,1,0:T(8,128)(2,1)S(1)}, bf16[4,4,64,128]{3,2,1,0:T(8,128)(2,1)}, u32[]{:S(2)}, u32[]{:S(2)}) collective-permute-start(bf16[4,4,64,128]{3,2,1,0:T(8,128)(2,1)S(1)} %bitcast.100), channel_id=1, source_target_pairs={{0,3},{1,2},{2,1},{3,0},{4,7},{5,6},{6,5},{7,4},{8,11},{9,10},{10,... | collective-permute-start | bytes 786440 | tf_op jit(solution)/shard_map/ppermute | solution.py:662
  79.5 29.3 %collective-permute-start.4 = (bf16[4,4,256,128]{3,2,1,0:T(8,128)(2,1)S(1)}, bf16[4,4,256,128]{3,2,1,0:T(8,128)(2,1)S(1)}, u32[]{:S(2)}, u32[]{:S(2)}) collective-permute-start(bf16[4,4,256,128]{3,2,1,0:T(8,128)(2,1)S(1)} %bitcast.70), channel_id=1, source_target_pairs={{0,16},{16,0},{1,17},{17,1},{2,18},{18,2},{3,19},{19,3},{4,20},{20... | collective-permute-start | bytes 3145736 | tf_op jit(solution)/shard_map/ppermute | solution.py:412
  81.1 27.7 %collective-permute-start.5 = (bf16[4,8,64,128]{3,2,1,0:T(8,128)(2,1)S(1)}, bf16[4,8,64,128]{3,2,1,0:T(8,128)(2,1)S(1)}, u32[]{:S(2)}, u32[]{:S(2)}) collective-permute-start(bf16[4,8,64,128]{3,2,1,0:T(8,128)(2,1)S(1)} %bitcast.79), channel_id=1, source_target_pairs={{0,2},{1,3},{2,0},{3,1},{4,6},{5,7},{6,4},{7,5},{8,10},{9,11},{10,... | collective-permute-start | bytes 1572872 | tf_op jit(solution)/shard_map/ppermute | solution.py:662
  82.6 26.2 %collective-permute-start.6 = (bf16[4,8,64,128]{3,2,1,0:T(8,128)(2,1)S(1)}, bf16[4,8,64,128]{3,2,1,0:T(8,128)(2,1)}, u32[]{:S(2)}, u32[]{:S(2)}) collective-permute-start(bf16[4,8,64,128]{3,2,1,0:T(8,128)(2,1)S(1)} %bitcast.80), channel_id=1, source_target_pairs={{0,1},{1,0},{2,3},{3,2},{4,5},{5,4},{6,7},{7,6},{8,9},{9,8},{10,11... | collective-permute-start | bytes 1572872 | tf_op jit(solution)/shard_map/ppermute | solution.py:662
  82.6 26.2 %collective-permute-start.7 = (bf16[4,8,64,128]{3,2,1,0:T(8,128)(2,1)S(1)}, bf16[4,8,64,128]{3,2,1,0:T(8,128)(2,1)}, u32[]{:S(2)}, u32[]{:S(2)}) collective-permute-start(bf16[4,8,64,128]{3,2,1,0:T(8,128)(2,1)S(1)} %bitcast.81), channel_id=1, source_target_pairs={{0,3},{1,2},{2,1},{3,0},{4,7},{5,6},{6,5},{7,4},{8,11},{9,10},{10,... | collective-permute-start | bytes 1572872 | tf_op jit(solution)/shard_map/ppermute | solution.py:662
  108.8 15.6 %collective-permute-start.8 = (bf16[4,80,512]{2,1,0:T(8,128)(2,1)}, bf16[4,80,512]{2,1,0:T(8,128)(2,1)S(1)}, u32[]{:S(2)}, u32[]{:S(2)}) collective-permute-start(bf16[4,80,512]{2,1,0:T(8,128)(2,1)} %get-tuple-element.140), channel_id=1, source_target_pairs={{0,2},{1,3},{2,0},{3,1},{4,6},{5,7},{6,4},{7,5},{8,10},{9,11},{10,... | collective-permute-start | bytes 983048 | tf_op jit(solution)/shard_map/ppermute | solution.py:662
  110.4 14.0 %collective-permute-start.9 = (bf16[4,80,512]{2,1,0:T(8,128)(2,1)}, bf16[4,80,512]{2,1,0:T(8,128)(2,1)S(1)}, u32[]{:S(2)}, u32[]{:S(2)}) collective-permute-start(bf16[4,80,512]{2,1,0:T(8,128)(2,1)} %get-tuple-element.141), channel_id=1, source_target_pairs={{0,1},{1,0},{2,3},{3,2},{4,5},{5,4},{6,7},{7,6},{8,9},{9,8},{10,11... | collective-permute-start | bytes 983048 | tf_op jit(solution)/shard_map/ppermute | solution.py:662
  111.7 15.0 %collective-permute-start.10 = (bf16[4,80,512]{2,1,0:T(8,128)(2,1)}, bf16[4,80,512]{2,1,0:T(8,128)(2,1)S(1)}, u32[]{:S(2)}, u32[]{:S(2)}) collective-permute-start(bf16[4,80,512]{2,1,0:T(8,128)(2,1)} %get-tuple-element.142), channel_id=1, source_target_pairs={{0,3},{1,2},{2,1},{3,0},{4,7},{5,6},{6,5},{7,4},{8,11},{9,10},{10,... | collective-permute-start | bytes 983048 | tf_op jit(solution)/shard_map/ppermute | solution.py:662
  129.9 35.2 %all-to-all-start.2 = ((bf16[4,64,512]{2,1,0:T(8,128)(2,1)}), bf16[4,64,512]{2,1,0:T(8,128)(2,1)S(1)}, u32[]{:S(2)}, u32[]{:S(2)}) async-start(bf16[4,64,512]{2,1,0:T(8,128)(2,1)} %get-tuple-element.143.refs_11_), calls=%async_computation.2 | async-start | bytes 524288 | tf_op jit(solution)/shard_map/all_to_all | solution.py:654
  145.9 14.6 %collective-permute-start.11 = (bf16[4,80,512]{2,1,0:T(8,128)(2,1)}, bf16[4,80,512]{2,1,0:T(8,128)(2,1)S(1)}, u32[]{:S(2)}, u32[]{:S(2)}) collective-permute-start(bf16[4,80,512]{2,1,0:T(8,128)(2,1)} %get-tuple-element.151), channel_id=1, source_target_pairs={{0,2},{1,3},{2,0},{3,1},{4,6},{5,7},{6,4},{7,5},{8,10},{9,11},{10,... | collective-permute-start | bytes 983048 | tf_op jit(solution)/shard_map/ppermute | solution.py:662
  147.4 13.1 %collective-permute-start.12 = (bf16[4,80,512]{2,1,0:T(8,128)(2,1)}, bf16[4,80,512]{2,1,0:T(8,128)(2,1)S(1)}, u32[]{:S(2)}, u32[]{:S(2)}) collective-permute-start(bf16[4,80,512]{2,1,0:T(8,128)(2,1)} %get-tuple-element.152), channel_id=1, source_target_pairs={{0,1},{1,0},{2,3},{3,2},{4,5},{5,4},{6,7},{7,6},{8,9},{9,8},{10,11... | collective-permute-start | bytes 983048 | tf_op jit(solution)/shard_map/ppermute | solution.py:662
  147.4 14.5 %collective-permute-start.13 = (bf16[4,80,512]{2,1,0:T(8,128)(2,1)}, bf16[4,80,512]{2,1,0:T(8,128)(2,1)S(1)}, u32[]{:S(2)}, u32[]{:S(2)}) collective-permute-start(bf16[4,80,512]{2,1,0:T(8,128)(2,1)} %get-tuple-element.153), channel_id=1, source_target_pairs={{0,3},{1,2},{2,1},{3,0},{4,7},{5,6},{6,5},{7,4},{8,11},{9,10},{10,... | collective-permute-start | bytes 983048 | tf_op jit(solution)/shard_map/ppermute | solution.py:662
  165.2 36.9 %all-to-all-start.3 = ((bf16[4,64,512]{2,1,0:T(8,128)(2,1)}), bf16[4,64,512]{2,1,0:T(8,128)(2,1)S(1)}, u32[]{:S(2)}, u32[]{:S(2)}) async-start(bf16[4,64,512]{2,1,0:T(8,128)(2,1)} %get-tuple-element.154.refs_11_), calls=%async_computation.3 | async-start | bytes 524288 | tf_op jit(solution)/shard_map/all_to_all | solution.py:654
  182.4 10.8 %collective-permute-start.14 = (bf16[4,80,512]{2,1,0:T(8,128)(2,1)}, bf16[4,80,512]{2,1,0:T(8,128)(2,1)S(1)}, u32[]{:S(2)}, u32[]{:S(2)}) collective-permute-start(bf16[4,80,512]{2,1,0:T(8,128)(2,1)} %get-tuple-element.161), channel_id=1, source_target_pairs={{0,2},{1,3},{2,0},{3,1},{4,6},{5,7},{6,4},{7,5},{8,10},{9,11},{10,... | collective-permute-start | bytes 983048 | tf_op jit(solution)/shard_map/ppermute | solution.py:662
  183.6 9.6 %collective-permute-start.15 = (bf16[4,80,512]{2,1,0:T(8,128)(2,1)}, bf16[4,80,512]{2,1,0:T(8,128)(2,1)S(1)}, u32[]{:S(2)}, u32[]{:S(2)}) collective-permute-start(bf16[4,80,512]{2,1,0:T(8,128)(2,1)} %get-tuple-element.162), channel_id=1, source_target_pairs={{0,1},{1,0},{2,3},{3,2},{4,5},{5,4},{6,7},{7,6},{8,9},{9,8},{10,11... | collective-permute-start | bytes 983048 | tf_op jit(solution)/shard_map/ppermute | solution.py:662
  184.1 14.8 %collective-permute-start.16 = (bf16[4,80,512]{2,1,0:T(8,128)(2,1)}, bf16[4,80,512]{2,1,0:T(8,128)(2,1)S(1)}, u32[]{:S(2)}, u32[]{:S(2)}) collective-permute-start(bf16[4,80,512]{2,1,0:T(8,128)(2,1)} %get-tuple-element.163), channel_id=1, source_target_pairs={{0,3},{1,2},{2,1},{3,0},{4,7},{5,6},{6,5},{7,4},{8,11},{9,10},{10,... | collective-permute-start | bytes 983048 | tf_op jit(solution)/shard_map/ppermute | solution.py:662
  202.1 14.3 %all-to-all-start.4 = ((bf16[4,64,512]{2,1,0:T(8,128)(2,1)}), bf16[4,64,512]{2,1,0:T(8,128)(2,1)S(1)}, u32[]{:S(2)}, u32[]{:S(2)}) async-start(bf16[4,64,512]{2,1,0:T(8,128)(2,1)} %get-tuple-element.164), calls=%async_computation.4 | async-start | bytes 524288 | tf_op jit(solution)/shard_map/all_to_all | solution.py:654
  239.7 30.0 %all-to-all-start.5 = ((bf16[4,192,512]{2,1,0:T(8,128)(2,1)}), bf16[4,192,512]{2,1,0:T(8,128)(2,1)S(1)}, u32[]{:S(2)}, u32[]{:S(2)}) async-start(bf16[4,192,512]{2,1,0:T(8,128)(2,1)} %get-tuple-element.167), calls=%async_computation.5 | async-start | bytes 1572864 | tf_op jit(solution)/shard_map/all_to_all | solution.py:654
  243.2 68.7 %reduce-scatter.6.cloned.1.call-start = ((), (), s32[]{:S(2)}) async-start(), calls=%async_computation.13 | async-start | bytes 21430272 | tf_op jit(solution)/shard_map/reduce_scatter | solution.py:845
  273.3 256.5 %reduce-scatter.10.cloned.1.call-start = ((), (), s32[]{:S(2)}) async-start(), calls=%async_computation.15 | async-start | bytes 8929280
  312.8 28.6 %collective-permute-start.20 = (bf16[4,80,512]{2,1,0:T(8,128)(2,1)S(1)}, bf16[4,80,512]{2,1,0:T(8,128)(2,1)S(1)}, u32[]{:S(2)}, u32[]{:S(2)}) collective-permute-start(bf16[4,80,512]{2,1,0:T(8,128)(2,1)S(1)} %copy-done.35), channel_id=1, source_target_pairs={{0,2},{1,3},{2,0},{3,1},{4,6},{5,7},{6,4},{7,5},{8,10},{9,11},{10,... | collective-permute-start | bytes 983048 | tf_op jit(solution)/shard_map/ppermute | solution.py:662
  314.0 27.4 %collective-permute-start.21 = (bf16[4,80,512]{2,1,0:T(8,128)(2,1)S(1)}, bf16[4,80,512]{2,1,0:T(8,128)(2,1)S(1)}, u32[]{:S(2)}, u32[]{:S(2)}) collective-permute-start(bf16[4,80,512]{2,1,0:T(8,128)(2,1)S(1)} %copy-done.35), channel_id=1, source_target_pairs={{0,1},{1,0},{2,3},{3,2},{4,5},{5,4},{6,7},{7,6},{8,9},{9,8},{10,11... | collective-permute-start | bytes 983048 | tf_op jit(solution)/shard_map/ppermute | solution.py:662
  314.0 27.4 %collective-permute-start.22 = (bf16[4,80,512]{2,1,0:T(8,128)(2,1)S(1)}, bf16[4,80,512]{2,1,0:T(8,128)(2,1)S(1)}, u32[]{:S(2)}, u32[]{:S(2)}) collective-permute-start(bf16[4,80,512]{2,1,0:T(8,128)(2,1)S(1)} %copy-done.35), channel_id=1, source_target_pairs={{0,3},{1,2},{2,1},{3,0},{4,7},{5,6},{6,5},{7,4},{8,11},{9,10},{10,... | collective-permute-start | bytes 983048 | tf_op jit(solution)/shard_map/ppermute | solution.py:662
  341.5 29.5 %collective-permute-start.23 = (bf16[4,2,256,128]{3,2,1,0:T(8,128)(2,1)}, bf16[4,2,256,128]{3,2,1,0:T(8,128)(2,1)S(1)}, u32[]{:S(2)}, u32[]{:S(2)}) collective-permute-start(bf16[4,2,256,128]{3,2,1,0:T(8,128)(2,1)} %bitcast.119), channel_id=1, source_target_pairs={{0,16},{16,0},{1,17},{17,1},{2,18},{18,2},{3,19},{19,3},{4,20},{20... | collective-permute-start | bytes 1572872 | tf_op jit(solution)/shard_map/ppermute | solution.py:412
  342.0 28.9 %collective-permute-start.24 = (bf16[4,64,512]{2,1,0:T(8,128)(2,1)}, bf16[4,64,512]{2,1,0:T(8,128)(2,1)S(1)}, u32[]{:S(2)}, u32[]{:S(2)}) collective-permute-start(bf16[4,64,512]{2,1,0:T(8,128)(2,1)} %get-tuple-element.201), channel_id=1, source_target_pairs={{0,2},{1,3},{2,0},{3,1},{4,6},{5,7},{6,4},{7,5},{8,10},{9,11},{10,... | collective-permute-start | bytes 786440 | tf_op jit(solution)/shard_map/ppermute | solution.py:662
  343.7 27.3 %collective-permute-start.25 = (bf16[4,64,512]{2,1,0:T(8,128)(2,1)}, bf16[4,64,512]{2,1,0:T(8,128)(2,1)S(1)}, u32[]{:S(2)}, u32[]{:S(2)}) collective-permute-start(bf16[4,64,512]{2,1,0:T(8,128)(2,1)} %get-tuple-element.202), channel_id=1, source_target_pairs={{0,1},{1,0},{2,3},{3,2},{4,5},{5,4},{6,7},{7,6},{8,9},{9,8},{10,11... | collective-permute-start | bytes 786440 | tf_op jit(solution)/shard_map/ppermute | solution.py:662
  343.7 27.3 %collective-permute-start.26 = (bf16[4,64,512]{2,1,0:T(8,128)(2,1)}, bf16[4,64,512]{2,1,0:T(8,128)(2,1)S(1)}, u32[]{:S(2)}, u32[]{:S(2)}) collective-permute-start(bf16[4,64,512]{2,1,0:T(8,128)(2,1)} %get-tuple-element.203), channel_id=1, source_target_pairs={{0,3},{1,2},{2,1},{3,0},{4,7},{5,6},{6,5},{7,4},{8,11},{9,10},{10,... | collective-permute-start | bytes 786440 | tf_op jit(solution)/shard_map/ppermute | solution.py:662
  374.7 66.9 %all-to-all-start.6 = ((bf16[4,768,128]{2,1,0:T(8,128)(2,1)}), bf16[4,768,128]{2,1,0:T(8,128)(2,1)S(1)}, u32[]{:S(2)}, u32[]{:S(2)}) async-start(bf16[4,768,128]{2,1,0:T(8,128)(2,1)} %shard_map.217.refs_17_), calls=%async_computation.7 | async-start | bytes 1572864 | tf_op jit(solution)/shard_map/all_to_all | solution.py:654
  379.2 28.6 %collective-permute-start.27 = (bf16[4,80,512]{2,1,0:T(8,128)(2,1)S(1)}, bf16[4,80,512]{2,1,0:T(8,128)(2,1)S(1)}, u32[]{:S(2)}, u32[]{:S(2)}) collective-permute-start(bf16[4,80,512]{2,1,0:T(8,128)(2,1)S(1)} %copy-done.34), channel_id=1, source_target_pairs={{0,2},{1,3},{2,0},{3,1},{4,6},{5,7},{6,4},{7,5},{8,10},{9,11},{10,... | collective-permute-start | bytes 983048 | tf_op jit(solution)/shard_map/ppermute | solution.py:662
  380.9 27.0 %collective-permute-start.28 = (bf16[4,80,512]{2,1,0:T(8,128)(2,1)S(1)}, bf16[4,80,512]{2,1,0:T(8,128)(2,1)S(1)}, u32[]{:S(2)}, u32[]{:S(2)}) collective-permute-start(bf16[4,80,512]{2,1,0:T(8,128)(2,1)S(1)} %copy-done.34), channel_id=1, source_target_pairs={{0,1},{1,0},{2,3},{3,2},{4,5},{5,4},{6,7},{7,6},{8,9},{9,8},{10,11... | collective-permute-start | bytes 983048 | tf_op jit(solution)/shard_map/ppermute | solution.py:662
  380.9 27.0 %collective-permute-start.29 = (bf16[4,80,512]{2,1,0:T(8,128)(2,1)S(1)}, bf16[4,80,512]{2,1,0:T(8,128)(2,1)S(1)}, u32[]{:S(2)}, u32[]{:S(2)}) collective-permute-start(bf16[4,80,512]{2,1,0:T(8,128)(2,1)S(1)} %copy-done.34), channel_id=1, source_target_pairs={{0,3},{1,2},{2,1},{3,0},{4,7},{5,6},{6,5},{7,4},{8,11},{9,10},{10,... | collective-permute-start | bytes 983048 | tf_op jit(solution)/shard_map/ppermute | solution.py:662
  407.9 30.1 %collective-permute-start.30 = (bf16[4,2,256,128]{3,2,1,0:T(8,128)(2,1)}, bf16[4,2,256,128]{3,2,1,0:T(8,128)(2,1)S(1)}, u32[]{:S(2)}, u32[]{:S(2)}) collective-permute-start(bf16[4,2,256,128]{3,2,1,0:T(8,128)(2,1)} %bitcast.117), channel_id=1, source_target_pairs={{0,16},{16,0},{1,17},{17,1},{2,18},{18,2},{3,19},{19,3},{4,20},{20... | collective-permute-start | bytes 1572872 | tf_op jit(solution)/shard_map/ppermute | solution.py:412
  409.1 28.8 %collective-permute-start.31 = (bf16[4,64,512]{2,1,0:T(8,128)(2,1)}, bf16[4,64,512]{2,1,0:T(8,128)(2,1)S(1)}, u32[]{:S(2)}, u32[]{:S(2)}) collective-permute-start(bf16[4,64,512]{2,1,0:T(8,128)(2,1)} %get-tuple-element.223), channel_id=1, source_target_pairs={{0,2},{1,3},{2,0},{3,1},{4,6},{5,7},{6,4},{7,5},{8,10},{9,11},{10,... | collective-permute-start | bytes 786440 | tf_op jit(solution)/shard_map/ppermute | solution.py:662
  410.7 27.2 %collective-permute-start.32 = (bf16[4,64,512]{2,1,0:T(8,128)(2,1)}, bf16[4,64,512]{2,1,0:T(8,128)(2,1)S(1)}, u32[]{:S(2)}, u32[]{:S(2)}) collective-permute-start(bf16[4,64,512]{2,1,0:T(8,128)(2,1)} %get-tuple-element.224), channel_id=1, source_target_pairs={{0,1},{1,0},{2,3},{3,2},{4,5},{5,4},{6,7},{7,6},{8,9},{9,8},{10,11... | collective-permute-start | bytes 786440 | tf_op jit(solution)/shard_map/ppermute | solution.py:662
  410.7 27.3 %collective-permute-start.33 = (bf16[4,64,512]{2,1,0:T(8,128)(2,1)}, bf16[4,64,512]{2,1,0:T(8,128)(2,1)S(1)}, u32[]{:S(2)}, u32[]{:S(2)}) collective-permute-start(bf16[4,64,512]{2,1,0:T(8,128)(2,1)} %get-tuple-element.225), channel_id=1, source_target_pairs={{0,3},{1,2},{2,1},{3,0},{4,7},{5,6},{6,5},{7,4},{8,11},{9,10},{10,... | collective-permute-start | bytes 786440 | tf_op jit(solution)/shard_map/ppermute | solution.py:662
  441.6 48.9 %all-to-all-start.7 = ((bf16[4,768,128]{2,1,0:T(8,128)(2,1)}), bf16[4,768,128]{2,1,0:T(8,128)(2,1)S(1)}, u32[]{:S(2)}, u32[]{:S(2)}) async-start(bf16[4,768,128]{2,1,0:T(8,128)(2,1)} %shard_map.220.refs_17_), calls=%async_computation.8 | async-start | bytes 1572864 | tf_op jit(solution)/shard_map/all_to_all | solution.py:654
  446.7 121.1 %reduce-scatter.8.cloned.1.call-start = ((), (), s32[]{:S(2)}) async-start(), calls=%async_computation.14 | async-start | bytes 2232320 | tf_op jit(solution)/shard_map/reduce_scatter | solution.py:878
  473.2 13.8 %collective-permute-start.34 = (bf16[4,2,256,128]{3,2,1,0:T(8,128)(2,1)}, bf16[4,2,256,128]{3,2,1,0:T(8,128)(2,1)S(1)}, u32[]{:S(2)}, u32[]{:S(2)}) collective-permute-start(bf16[4,2,256,128]{3,2,1,0:T(8,128)(2,1)} %bitcast.118), channel_id=1, source_target_pairs={{0,16},{16,0},{1,17},{17,1},{2,18},{18,2},{3,19},{19,3},{4,20},{20... | collective-permute-start | bytes 1572872 | tf_op jit(solution)/shard_map/ppermute | solution.py:412
  474.1 9.5 %collective-permute-start.35 = (bf16[4,64,512]{2,1,0:T(8,128)(2,1)}, bf16[4,64,512]{2,1,0:T(8,128)(2,1)S(1)}, u32[]{:S(2)}, u32[]{:S(2)}) collective-permute-start(bf16[4,64,512]{2,1,0:T(8,128)(2,1)} %get-tuple-element.236), channel_id=1, source_target_pairs={{0,2},{1,3},{2,0},{3,1},{4,6},{5,7},{6,4},{7,5},{8,10},{9,11},{10,... | collective-permute-start | bytes 786440 | tf_op jit(solution)/shard_map/ppermute | solution.py:662
  475.8 7.8 %collective-permute-start.36 = (bf16[4,64,512]{2,1,0:T(8,128)(2,1)}, bf16[4,64,512]{2,1,0:T(8,128)(2,1)S(1)}, u32[]{:S(2)}, u32[]{:S(2)}) collective-permute-start(bf16[4,64,512]{2,1,0:T(8,128)(2,1)} %get-tuple-element.237), channel_id=1, source_target_pairs={{0,1},{1,0},{2,3},{3,2},{4,5},{5,4},{6,7},{7,6},{8,9},{9,8},{10,11... | collective-permute-start | bytes 786440 | tf_op jit(solution)/shard_map/ppermute | solution.py:662
  475.8 11.1 %collective-permute-start.37 = (bf16[4,64,512]{2,1,0:T(8,128)(2,1)}, bf16[4,64,512]{2,1,0:T(8,128)(2,1)S(1)}, u32[]{:S(2)}, u32[]{:S(2)}) collective-permute-start(bf16[4,64,512]{2,1,0:T(8,128)(2,1)} %get-tuple-element.238), channel_id=1, source_target_pairs={{0,3},{1,2},{2,1},{3,0},{4,7},{5,6},{6,5},{7,4},{8,11},{9,10},{10,... | collective-permute-start | bytes 786440 | tf_op jit(solution)/shard_map/ppermute | solution.py:662
  536.4 12.5 %collective-permute-start.41 = (bf16[2,2,448,128]{3,2,0,1:T(8,128)(2,1)S(1)}, bf16[2,2,448,128]{3,2,0,1:T(8,128)(2,1)S(1)}, u32[]{:S(2)}, u32[]{:S(2)}) collective-permute-start(bf16[2,2,448,128]{3,2,0,1:T(8,128)(2,1)S(1)} %bitcast.96), channel_id=1, source_target_pairs={{0,16},{16,0},{1,17},{17,1},{2,18},{18,2},{3,19},{19,3},{4,20},{20... | collective-permute-start | bytes 1376264 | tf_op jit(solution)/shard_map/ppermute | solution.py:412
  537.4 13.2 %collective-permute-start.39 = (bf16[2,2,448,128]{3,2,0,1:T(8,128)(2,1)S(1)}, bf16[2,2,448,128]{3,2,0,1:T(8,128)(2,1)S(1)}, u32[]{:S(2)}, u32[]{:S(2)}) collective-permute-start(bf16[2,2,448,128]{3,2,0,1:T(8,128)(2,1)S(1)} %bitcast.97), channel_id=1, source_target_pairs={{0,2},{2,0},{1,3},{3,1},{4,6},{6,4},{5,7},{7,5},{8,10},{10,8},{9,1... | collective-permute-start | bytes 1376264 | tf_op jit(solution)/shard_map/ppermute | solution.py:412
  584.9 8.6 %collective-permute-start.43 = (bf16[448,128]{1,0:T(8,128)(2,1)S(1)}, bf16[448,128]{1,0:T(8,128)(2,1)S(1)}, u32[]{:S(2)}, u32[]{:S(2)}) collective-permute-start(bf16[448,128]{1,0:T(8,128)(2,1)S(1)} %fusion.5), channel_id=1, source_target_pairs={{8,4},{12,0},{9,5},{13,1},{10,6},{14,2},{11,7},{15,3},{24,20},{28,... | collective-permute-start | bytes 344072 | tf_op jit(solution)/shard_map/ppermute | solution.py:437
  (53 other events, 357.8 us)
Sparse Core Ops, SparseCore 0:
  273.5 23.9 reduce-scatter.5
  312.0 107.3 reduce-scatter.9
  530.0 37.7 reduce-scatter.7
